TPU v7x, 32 devices: a whole 2x2x4 slice. The times are simulated.
32 devices in a mesh: dp: 4 (over x, core), seq: 2 (over y), mp: 4 (over z).
Axes of the slice: x: 2, y: 2, z: 4, core: 2. Of those that a mesh axis runs over, the one named last changes fastest.
Arguments:
- tokens: bfloat16 [8, 1024, 2048], P('dp', 'seq'), may hold values from -6 to 6
- block_ids: int32 [8, 1024], P('dp'), may hold values from 0 to 7, never falling along the last dimension, each value on 1 to 256 neighbouring positions
- query_weight: bfloat16 [2048, 2048], P(('dp', 'seq'), 'mp'), may hold values from -0.125 to 0.125
- key_weight: bfloat16 [2048, 2048], P(('dp', 'seq'), 'mp'), may hold values from -0.125 to 0.125
- value_weight: bfloat16 [2048, 2048], P(('dp', 'seq'), 'mp'), may hold values from -0.125 to 0.125
- out_weight: bfloat16 [2048, 2048], P(('dp', 'seq'), 'mp'), may hold values from -2 to 2
- gate_weight: bfloat16 [2048, 8192], P(('dp', 'seq'), 'mp'), may hold values from -0.125 to 0.125
- up_weight: bfloat16 [2048, 8192], P(('dp', 'seq'), 'mp'), may hold values from -0.125 to 0.125
- down_weight: bfloat16 [2048, 8192], P(('dp', 'seq'), 'mp'), may hold values from -0.0625 to 0.0625
- out_grad: bfloat16 [8, 1024, 2048], P('dp', 'seq'), may hold values from -6 to 6
Outputs:
- output: bfloat16 [8, 1024, 2048], P('dp', 'seq')
- tokens_grad: bfloat16 [8, 1024, 2048], P('dp', 'seq')
- query_grad: float32 [2048, 2048], P(('dp', 'seq'), 'mp')
- key_grad: float32 [2048, 2048], P(('dp', 'seq'), 'mp')
- value_grad: float32 [2048, 2048], P(('dp', 'seq'), 'mp')
- out_weight_grad: float32 [2048, 2048], P(('dp', 'seq'), 'mp')
- gate_grad: float32 [2048, 8192], P(('dp', 'seq'), 'mp')
- up_grad: float32 [2048, 8192], P(('dp', 'seq'), 'mp')
- down_grad: float32 [2048, 8192], P(('dp', 'seq'), 'mp')
Inputs may be any that keep to these rules, and one draw needn't show every extreme that they name: `block_ids`: along each sequence the block numbers never fall; every number from 0 to 7 appears; a block holds 1 to 256 positions and some block holds exactly 256.
All inputs are finite; a program needn't handle non-finite values.
Results may differ from a plain program's by a relative error of at most 0.023.
Values may be sent and summed in bfloat16 or wider, within the bound.
A program may use at most 256 MiB of HBM per device.

v0:
```python
import math

import jax
import jax.numpy as jnp
from jax import lax
from jax.sharding import PartitionSpec as P

HD = 128


EPSILON = 1e-05
THETA = 10000.0
MASKED = -1e30


def layer_norm(values):
    centered = values - jnp.mean(values, axis=-1, keepdims=True)
    inverse = lax.rsqrt(jnp.mean(centered * centered, axis=-1, keepdims=True) + EPSILON)
    return (centered * inverse, inverse)


def norm_back(normed, inverse, upstream):
    middle_term = upstream - jnp.mean(upstream, axis=-1, keepdims=True)
    return inverse * (middle_term - normed * jnp.mean(upstream * normed, axis=-1, keepdims=True))


def rope_tables(positions):
    steps_index = jnp.arange(HD // 2).astype(jnp.float32)
    frequency = jnp.exp(steps_index * (-2.0 * math.log(THETA) / HD))
    angles = positions[:, None] * frequency[None, :]
    cosine = jnp.concatenate([jnp.cos(angles), jnp.cos(angles)], axis=-1)
    sine_table = jnp.concatenate([jnp.sin(angles), jnp.sin(angles)], axis=-1)
    return (cosine, sine_table)


def rotate(values, cosine, sine_table):
    halfway = values.shape[-1] // 2
    turned = jnp.concatenate([-values[..., halfway:], values[..., :halfway]], axis=-1)
    return values * cosine + turned * sine_table


def unrotate(values, cosine, sine_table):
    halfway = values.shape[-1] // 2
    scaled = values * sine_table
    turned = jnp.concatenate([scaled[..., halfway:], -scaled[..., :halfway]], axis=-1)
    return values * cosine + turned


def matmul(factor_left, factor_right):
    return jnp.dot(factor_left, factor_right, preferred_element_type=jnp.float32)


def matmul_trans(factor_left, factor_right):
    return lax.dot_general(
        factor_left, factor_right, (((1,), (1,)), ((), ())), preferred_element_type=jnp.float32
    )


def outer_sum(factor_left, factor_right):
    return lax.dot_general(
        factor_left, factor_right, (((0,), (0,)), ((), ())), preferred_element_type=jnp.float32
    )


def body(
    tokens,
    block_ids,
    query_weight,
    key_weight,
    value_weight,
    out_weight,
    gate_weight,
    up_weight,
    down_weight,
    out_grad,
):
    groups, shard_len, model_width = tokens.shape
    seq_rank = lax.axis_index("seq")
    seq_len = shard_len * lax.axis_size("seq")
    row_count = groups * shard_len
    shards = (
        query_weight,
        key_weight,
        value_weight,
        out_weight,
        gate_weight,
        up_weight,
        down_weight,
    )
    full_query, full_key, full_value, full_out, full_gate, full_up, full_down = (
        lax.all_gather(shards[0], ("dp", "seq"), axis=0, tiled=True),
        lax.all_gather(shards[1], ("dp", "seq"), axis=0, tiled=True),
        lax.all_gather(shards[2], ("dp", "seq"), axis=0, tiled=True),
        lax.all_gather(shards[3], ("dp", "seq"), axis=0, tiled=True),
        lax.all_gather(shards[4], ("dp", "seq"), axis=0, tiled=True),
        lax.all_gather(shards[5], ("dp", "seq"), axis=0, tiled=True),
        lax.all_gather(shards[6], ("dp", "seq"), axis=0, tiled=True),
    )
    heads_here = full_query.shape[1] // HD
    shape_heads = (groups, shard_len, heads_here, HD)
    score_root = math.sqrt(HD)
    positions = (seq_rank * shard_len + jnp.arange(shard_len)).astype(jnp.float32)
    cosine, sine_table = rope_tables(positions)
    cosine = cosine[None, :, None, :]
    sine_table = sine_table[None, :, None, :]
    inputs = tokens.astype(jnp.float32).reshape(row_count, model_width)
    normed, inverse = layer_norm(inputs)
    normed_low = normed.astype(jnp.bfloat16)
    queries = rotate(
        matmul(normed_low, full_query).reshape(shape_heads), cosine, sine_table
    ).astype(jnp.bfloat16)
    key_local = (
        rotate(matmul(normed_low, full_key).reshape(shape_heads), cosine, sine_table)
        .astype(jnp.bfloat16)
        .reshape(groups, shard_len, -1)
    )
    value_local = matmul(normed_low, full_value).astype(jnp.bfloat16).reshape(groups, shard_len, -1)
    keys_all, values_all = (
        lax.all_gather(key_local, "seq", axis=1, tiled=True),
        lax.all_gather(value_local, "seq", axis=1, tiled=True),
    )
    query_ids = lax.dynamic_slice_in_dim(block_ids, seq_rank * shard_len, shard_len, 1)
    last_ids = query_ids[:, shard_len - 1 :]
    reached = jnp.sum((block_ids <= last_ids).astype(jnp.int32), axis=1)
    key_blocks = (jnp.max(reached) + shard_len - 1) // shard_len

    def block_scores(keys_source, offset):
        key_block = lax.dynamic_slice_in_dim(keys_source, offset, shard_len, 1).reshape(shape_heads)
        raw_scores = jnp.einsum(
            "gqhd,gkhd->ghqk", queries, key_block, preferred_element_type=jnp.float32
        )
        key_ids = lax.dynamic_slice_in_dim(block_ids, offset, shard_len, 1)
        allowed = key_ids[:, None, None, :] <= query_ids[:, None, :, None]
        return (jnp.where(allowed, raw_scores / score_root, MASKED), allowed, key_block)

    def stats_step(block_index, loop_state):
        running_max, running_sum = loop_state
        scores, allowed, key_block = block_scores(keys_all, block_index * shard_len)
        new_max = jnp.maximum(running_max, jnp.max(scores, axis=-1))
        weights_block = jnp.where(allowed, jnp.exp(scores - new_max[..., None]), 0.0)
        return (
            new_max,
            running_sum * jnp.exp(running_max - new_max) + jnp.sum(weights_block, axis=-1),
        )

    stat_shape = (groups, heads_here, shard_len)
    running_max, running_sum = lax.fori_loop(
        0,
        key_blocks,
        stats_step,
        (jnp.full(stat_shape, MASKED, jnp.float32), jnp.zeros(stat_shape, jnp.float32)),
    )
    log_total = running_max + jnp.log(running_sum)

    def output_step(block_index, accumulated):
        offset = block_index * shard_len
        scores, allowed, key_block = block_scores(keys_all, offset)
        weights_block = jnp.where(allowed, jnp.exp(scores - log_total[..., None]), 0.0).astype(
            jnp.bfloat16
        )
        value_block = lax.dynamic_slice_in_dim(values_all, offset, shard_len, 1).reshape(
            shape_heads
        )
        return accumulated + jnp.einsum(
            "ghqk,gkhd->gqhd", weights_block, value_block, preferred_element_type=jnp.float32
        )

    attended = lax.fori_loop(0, key_blocks, output_step, jnp.zeros(shape_heads, jnp.float32))
    attended_low = attended.astype(jnp.bfloat16).reshape(row_count, -1)
    branch = lax.psum(matmul_trans(attended_low, full_out).astype(jnp.bfloat16), "mp").astype(
        jnp.float32
    )
    middle = inputs + branch
    normed_two, inverse_two = layer_norm(middle)
    normed_two_low = normed_two.astype(jnp.bfloat16)
    gate_values = matmul(normed_two_low, full_gate)
    up_values = matmul(normed_two_low, full_up)
    sigmoid_gate = jax.nn.sigmoid(gate_values)
    activated = gate_values * sigmoid_gate
    hidden_low = (activated * up_values).astype(jnp.bfloat16)
    feed_out = lax.psum(matmul_trans(hidden_low, full_down).astype(jnp.bfloat16), "mp").astype(
        jnp.float32
    )
    output = (middle + feed_out).astype(jnp.bfloat16).reshape(groups, shard_len, model_width)
    full_query, full_key, full_value, full_out, full_gate, full_up, full_down = (
        lax.all_gather(shards[0], ("dp", "seq"), axis=0, tiled=True),
        lax.all_gather(shards[1], ("dp", "seq"), axis=0, tiled=True),
        lax.all_gather(shards[2], ("dp", "seq"), axis=0, tiled=True),
        lax.all_gather(shards[3], ("dp", "seq"), axis=0, tiled=True),
        lax.all_gather(shards[4], ("dp", "seq"), axis=0, tiled=True),
        lax.all_gather(shards[5], ("dp", "seq"), axis=0, tiled=True),
        lax.all_gather(shards[6], ("dp", "seq"), axis=0, tiled=True),
    )
    grad_low = out_grad.reshape(row_count, model_width)
    down_term = outer_sum(grad_low, hidden_low)
    grad_hidden = matmul(grad_low, full_down)
    grad_gate = (
        grad_hidden * up_values * sigmoid_gate * (1.0 + gate_values * (1.0 - sigmoid_gate))
    ).astype(jnp.bfloat16)
    grad_up = (grad_hidden * activated).astype(jnp.bfloat16)
    gate_term = outer_sum(normed_two_low, grad_gate)
    up_term = outer_sum(normed_two_low, grad_up)
    grad_normed_two = lax.psum(
        (matmul_trans(grad_gate, full_gate) + matmul_trans(grad_up, full_up)).astype(jnp.bfloat16),
        "mp",
    ).astype(jnp.float32)
    grad_middle = grad_low.astype(jnp.float32) + norm_back(normed_two, inverse_two, grad_normed_two)
    grad_branch = grad_middle.astype(jnp.bfloat16)
    out_term = outer_sum(grad_branch, attended_low)
    grad_attended = matmul(grad_branch, full_out).astype(jnp.bfloat16).reshape(shape_heads)
    row_delta = jnp.einsum("gqhd,gqhd->ghq", grad_attended.astype(jnp.float32), attended)

    def backward_step(block_index, loop_state):
        grad_queries, grad_keys, grad_values = loop_state
        offset = block_index * shard_len
        scores, allowed, key_block = block_scores(keys_all, offset)
        weights_block = jnp.where(allowed, jnp.exp(scores - log_total[..., None]), 0.0)
        value_block = lax.dynamic_slice_in_dim(values_all, offset, shard_len, 1).reshape(
            shape_heads
        )
        grad_weights = jnp.einsum(
            "gqhd,gkhd->ghqk", grad_attended, value_block, preferred_element_type=jnp.float32
        )
        grad_raw = (weights_block * (grad_weights - row_delta[..., None]) / score_root).astype(
            jnp.bfloat16
        )
        grad_queries = grad_queries + jnp.einsum(
            "ghqk,gkhd->gqhd", grad_raw, key_block, preferred_element_type=jnp.float32
        )
        key_part = jnp.einsum(
            "ghqk,gqhd->gkhd", grad_raw, queries, preferred_element_type=jnp.float32
        ).reshape(groups, shard_len, -1)
        value_part = jnp.einsum(
            "ghqk,gqhd->gkhd",
            weights_block.astype(jnp.bfloat16),
            grad_attended,
            preferred_element_type=jnp.float32,
        ).reshape(groups, shard_len, -1)
        grad_keys = lax.dynamic_update_slice_in_dim(grad_keys, key_part, offset, 1)
        grad_values = lax.dynamic_update_slice_in_dim(grad_values, value_part, offset, 1)
        return (grad_queries, grad_keys, grad_values)

    zero_full = jnp.zeros((groups, seq_len, heads_here * HD), jnp.float32)
    grad_queries, grad_keys, grad_values = lax.fori_loop(
        0, key_blocks, backward_step, (jnp.zeros(shape_heads, jnp.float32), zero_full, zero_full)
    )
    grad_key_sum, grad_value_sum = (
        lax.psum_scatter(
            grad_keys.astype(jnp.bfloat16), "seq", scatter_dimension=1, tiled=True
        ).astype(jnp.float32),
        lax.psum_scatter(
            grad_values.astype(jnp.bfloat16), "seq", scatter_dimension=1, tiled=True
        ).astype(jnp.float32),
    )
    grad_q_lin = (
        unrotate(grad_queries, cosine, sine_table).astype(jnp.bfloat16).reshape(row_count, -1)
    )
    grad_k_lin = (
        unrotate(grad_key_sum.reshape(shape_heads), cosine, sine_table)
        .astype(jnp.bfloat16)
        .reshape(row_count, -1)
    )
    grad_v_lin = grad_value_sum.astype(jnp.bfloat16).reshape(row_count, -1)
    query_term = outer_sum(normed_low, grad_q_lin)
    key_term = outer_sum(normed_low, grad_k_lin)
    value_term = outer_sum(normed_low, grad_v_lin)
    grad_partial = (
        matmul_trans(grad_q_lin, full_query)
        + matmul_trans(grad_k_lin, full_key)
        + matmul_trans(grad_v_lin, full_value)
    )
    grad_normed = lax.psum(grad_partial.astype(jnp.bfloat16), "mp").astype(jnp.float32)
    tokens_grad = (
        (grad_middle + norm_back(normed, inverse, grad_normed))
        .astype(jnp.bfloat16)
        .reshape(groups, shard_len, model_width)
    )
    grad_terms = (query_term, key_term, value_term, out_term, gate_term, up_term, down_term)
    query_grad, key_grad, value_grad, out_weight_grad, gate_grad, up_grad, down_grad = (
        lax.psum_scatter(
            grad_terms[0].astype(jnp.bfloat16), ("dp", "seq"), scatter_dimension=0, tiled=True
        ).astype(jnp.float32),
        lax.psum_scatter(
            grad_terms[1].astype(jnp.bfloat16), ("dp", "seq"), scatter_dimension=0, tiled=True
        ).astype(jnp.float32),
        lax.psum_scatter(
            grad_terms[2].astype(jnp.bfloat16), ("dp", "seq"), scatter_dimension=0, tiled=True
        ).astype(jnp.float32),
        lax.psum_scatter(
            grad_terms[3].astype(jnp.bfloat16), ("dp", "seq"), scatter_dimension=0, tiled=True
        ).astype(jnp.float32),
        lax.psum_scatter(
            grad_terms[4].astype(jnp.bfloat16), ("dp", "seq"), scatter_dimension=0, tiled=True
        ).astype(jnp.float32),
        lax.psum_scatter(
            grad_terms[5].astype(jnp.bfloat16), ("dp", "seq"), scatter_dimension=0, tiled=True
        ).astype(jnp.float32),
        lax.psum_scatter(
            grad_terms[6].astype(jnp.bfloat16), ("dp", "seq"), scatter_dimension=0, tiled=True
        ).astype(jnp.float32),
    )
    return (
        output,
        tokens_grad,
        query_grad,
        key_grad,
        value_grad,
        out_weight_grad,
        gate_grad,
        up_grad,
        down_grad,
    )


def solution(mesh):
    in_specs = (
        P("dp", "seq", None),
        P("dp", None),
        P(("dp", "seq"), "mp"),
        P(("dp", "seq"), "mp"),
        P(("dp", "seq"), "mp"),
        P(("dp", "seq"), "mp"),
        P(("dp", "seq"), "mp"),
        P(("dp", "seq"), "mp"),
        P(("dp", "seq"), "mp"),
        P("dp", "seq", None),
    )
    out_specs = (
        P("dp", "seq", None),
        P("dp", "seq", None),
        P(("dp", "seq"), "mp"),
        P(("dp", "seq"), "mp"),
        P(("dp", "seq"), "mp"),
        P(("dp", "seq"), "mp"),
        P(("dp", "seq"), "mp"),
        P(("dp", "seq"), "mp"),
        P(("dp", "seq"), "mp"),
    )
    return jax.shard_map(body, mesh=mesh, in_specs=in_specs, out_specs=out_specs, check_vma=False)
```

profile of v0, /device:TPU:0, one launch (start us, length us, event | category | flops | bytes accessed | tf_op | source)
XLA Modules:
  0.0 1614.6 jit_solution(9767359121337136558)
XLA Ops:
  19.5 21.0 %all-gather.18.cloned.1.call-done = bf16[2048,512]{1,0:T(8,128)(2,1)} async-done(((bf16[256,512]{1,0:T(8,128)(2,1)}), bf16[2048,512]{1,0:T(8,128)(2,1)}) %all-gather.18.cloned.1.call-update) | async-done | bytes 2097168 | tf_op jit(solution)/shard_map/all_gather | solution.py:91
  44.4 25.9 %all-gather.14.cloned.1.call-done = bf16[2048,512]{1,0:T(8,128)(2,1)} async-done(((bf16[256,512]{1,0:T(8,128)(2,1)}), bf16[2048,512]{1,0:T(8,128)(2,1)}) %all-gather.14.cloned.1.call-update) | async-done | bytes 2097168 | tf_op jit(solution)/shard_map/all_gather | solution.py:92
  111.2 24.1 %all-gather.16.cloned.1.call-done = bf16[2,1024,512]{1,2,0:T(8,128)(2,1)} async-done(((bf16[2,512,512]{1,2,0:T(8,128)(2,1)}), bf16[2,1024,512]{1,2,0:T(8,128)(2,1)}) %all-gather.16.cloned.1.call-update) | async-done | bytes 2097168 | tf_op jit(solution)/shard_map/all_gather | solution.py:119
  146.6 23.8 %all-gather.12.cloned.1.call-done = bf16[2,1024,512]{1,2,0:T(8,128)(2,1)} async-done(((bf16[2,512,512]{1,2,0:T(8,128)(2,1)}), bf16[2,1024,512]{1,2,0:T(8,128)(2,1)}) %all-gather.12.cloned.1.call-update) | async-done | bytes 2097168 | tf_op jit(solution)/shard_map/all_gather | solution.py:120
  172.0 16.9 %while.37 = (s32[]{:T(128)}, f32[2,512,4,128]{1,3,2,0:T(8,128)}, s32[]{:T(128)}, bf16[2,1024,512]{1,2,0:T(8,128)(2,1)}, s32[2,1024]{1,0:T(2,128)S(1)}, /*index=5...) while((s32[]{:T(128)}, f32[2,512,4,128]{1,3,2,0:T(8,128)}, ...), condition=%wide.region_9.10_spmd, body=%wide.region_8.9_spmd.sunk | while | flops 1085276160 | bytes 12615859 | solution.py:168
  208.6 152.6 %all-reduce.5.cloned.1.call-done = bf16[1024,2048]{1,0:T(8,128)(2,1)} async-done(((bf16[1024,2048]{1,0:T(8,128)(2,1)}), bf16[1024,2048]{1,0:T(8,128)(2,1)}) %all-reduce.5.cloned.1.call-update) | async-done | bytes 4194320 | tf_op jit(solution)/shard_map/psum | solution.py:170
  372.4 44.3 %all-gather.22.cloned.1.call-done = bf16[2048,2048]{1,0:T(8,128)(2,1)} async-done(((bf16[256,2048]{1,0:T(8,128)(2,1)}), bf16[2048,2048]{1,0:T(8,128)(2,1)}) %all-gather.22.cloned.1.call-update) | async-done | bytes 8388624 | tf_op jit(solution)/shard_map/all_gather | solution.py:95
  416.7 14.4 fusion.82
  431.1 42.1 %all-gather.24.cloned.1.call-done = bf16[2048,2048]{1,0:T(8,128)(2,1)} async-done(((bf16[256,2048]{1,0:T(8,128)(2,1)}), bf16[2048,2048]{1,0:T(8,128)(2,1)}) %all-gather.24.cloned.1.call-update) | async-done | bytes 8388624 | tf_op jit(solution)/shard_map/all_gather | solution.py:96
  473.2 14.4 fusion.83
  487.5 41.9 %all-gather.26.cloned.1.call-done = bf16[2048,2048]{1,0:T(8,128)(2,1)} async-done(((bf16[256,2048]{1,0:T(8,128)(2,1)}), bf16[2048,2048]{1,0:T(8,128)(2,1)}) %all-gather.26.cloned.1.call-update) | async-done | bytes 8388624 | tf_op jit(solution)/shard_map/all_gather | solution.py:97
  529.5 21.2 %multiply_convert_fusion = (bf16[1024,2048]{1,0:T(8,128)(2,1)S(1)}, bf16[1024,2048]{1,0:T(8,128)(2,1)}, bf16[1024,2048]{1,0:T(8,128)(2,1)}) fusion(f32[1024,2048]{1,0:T(8,128)} %fusion.82, f32[1024,2048]{1,0:T(8,128)} %fusion.83, bf16[1024,2048]{1,0:T(8,128)(2,1)} %bitcast.286, bf16[2048,2048]{1,0:T(8,128)(2,1)} %all-gather.26.cloned.1.call-done), kind=kOutput, calls=%fused_computation.73 | convolution fusion | flops 8621391872 | bytes 41943040 | tf_op jit(solution)/shard_map/dot_general | solution.py:50
  550.7 16.0 fusion.84
  579.2 155.1 %all-reduce.7.cloned.1.call-done = bf16[1024,2048]{1,0:T(8,128)(2,1)} async-done(((bf16[1024,2048]{1,0:T(8,128)(2,1)}), bf16[1024,2048]{1,0:T(8,128)(2,1)}) %all-reduce.7.cloned.1.call-update) | async-done | bytes 4194320 | tf_op jit(solution)/shard_map/psum | solution.py:203
  767.2 58.7 %while.38 = (s32[]{:T(128)}, f32[2,512,4,128]{1,3,2,0:T(8,128)}, bf16[2,1024,512]{2,1,0:T(8,128)(2,1)}, bf16[2,1024,512]{2,1,0:T(8,128)(2,1)}, s32[]{:T(128)}, /...) while((s32[]{:T(128)}, f32[2,512,4,128]{1,3,2,0:T(8,128)}, ...), condition=%wide.region_18.19_spmd, body=%wide.region_17.18_spmd.sunk | while | flops 2712666112 | bytes 147390880 | solution.py:244
  834.4 22.6 %reduce-scatter.10.cloned.1.call-done = bf16[2,512,512]{2,1,0:T(8,128)(2,1)} async-done(((bf16[2,1024,512]{2,1,0:T(8,128)(2,1)}), bf16[2,512,512]{2,1,0:T(8,128)(2,1)}) %reduce-scatter.10.cloned.1.call-update) | async-done | bytes 1048592 | tf_op jit(solution)/shard_map/reduce_scatter | solution.py:248
  898.0 14.3 convolution_convert_fusion.1
  926.7 14.1 convert_bitcast_fusion
  983.3 42.6 %reduce-scatter.16.cloned.1.call-done = bf16[256,512]{1,0:T(8,128)(2,1)} async-done(((bf16[2048,512]{1,0:T(8,128)(2,1)}), bf16[256,512]{1,0:T(8,128)(2,1)}) %reduce-scatter.16.cloned.1.call-update) | async-done | bytes 262160 | tf_op jit(solution)/shard_map/reduce_scatter | solution.py:283
  1027.7 43.5 %reduce-scatter.18.cloned.1.call-done = bf16[256,512]{1,0:T(8,128)(2,1)} async-done(((bf16[2048,512]{1,0:T(8,128)(2,1)}), bf16[256,512]{1,0:T(8,128)(2,1)}) %reduce-scatter.18.cloned.1.call-update) | async-done | bytes 262160 | tf_op jit(solution)/shard_map/reduce_scatter | solution.py:286
  1073.0 72.8 %reduce-scatter.22.cloned.1.call-done = bf16[256,2048]{1,0:T(8,128)(2,1)} async-done(((bf16[2048,2048]{1,0:T(8,128)(2,1)}), bf16[256,2048]{1,0:T(8,128)(2,1)}) %reduce-scatter.22.cloned.1.call-update) | async-done | bytes 1048592 | tf_op jit(solution)/shard_map/reduce_scatter | solution.py:292
  1148.6 72.4 %reduce-scatter.24.cloned.1.call-done = bf16[256,2048]{1,0:T(8,128)(2,1)} async-done(((bf16[2048,2048]{1,0:T(8,128)(2,1)}), bf16[256,2048]{1,0:T(8,128)(2,1)}) %reduce-scatter.24.cloned.1.call-update) | async-done | bytes 1048592 | tf_op jit(solution)/shard_map/reduce_scatter | solution.py:295
  1223.7 71.8 %reduce-scatter.26.cloned.1.call-done = bf16[256,2048]{0,1:T(8,128)(2,1)} async-done(((bf16[2048,2048]{0,1:T(8,128)(2,1)}), bf16[256,2048]{0,1:T(8,128)(2,1)}) %reduce-scatter.26.cloned.1.call-update) | async-done | bytes 1048592 | tf_op jit(solution)/shard_map/reduce_scatter | solution.py:298
  1298.1 292.3 %all-reduce.9.cloned.1.call-done = (bf16[1024,2048]{1,0:T(8,128)(2,1)}, bf16[1024,2048]{1,0:T(8,128)(2,1)}) async-done(((bf16[1024,2048]{1,0:T(8,128)(2,1)}, bf16[1024,2048]{1,0:T(8,128)(2,1)}), (bf16[1024,2048]{1,0:T(8,128)(2,1)}, bf16[1024,2048]{1,0:T(8,128)(2,1)})) %all-reduce.9.cloned.1.call-update) | async-done | bytes 8388624 | tf_op jit(solution)/shard_map/psum | solution.py:181
  (291 shorter events, 365.7 us)
Async XLA Ops:
  7.2 33.3 %all-gather.18.cloned.1.call-start = ((), (), s32[]{:S(2)}) async-start(), calls=%async_computation.13 | async-start | bytes 2359296 | tf_op jit(solution)/shard_map/all_gather | solution.py:91
  7.9 62.4 %all-gather.14.cloned.1.call-start = ((), (), s32[]{:S(2)}) async-start(), calls=%async_computation.11 | async-start | bytes 2359296 | tf_op jit(solution)/shard_map/all_gather | solution.py:92
  8.7 91.5 %all-gather.10.cloned.1.call-start = ((), (), s32[]{:S(2)}) async-start(), calls=%async_computation.9 | async-start | bytes 2359296 | tf_op jit(solution)/shard_map/all_gather | solution.py:93
  9.4 125.9 %all-gather.16.cloned.1.call-start = ((), (), s32[]{:S(2)}) async-start(), calls=%async_computation.12 | async-start | bytes 3145728 | tf_op jit(solution)/shard_map/all_gather | solution.py:119
  12.9 69.9 %copy-start.20 = (f32[512,128]{0,1:T(8,128)}, f32[512,128]{0,1:T(8,128)S(1)}, u32[]{:S(2)}) copy-start(f32[512,128]{0,1:T(8,128)S(1)} %get-tuple-element.353) | copy-start | bytes 786436
  85.0 85.4 %all-gather.12.cloned.1.call-start = ((), (), s32[]{:S(2)}) async-start(), calls=%async_computation.10 | async-start | bytes 3145728 | tf_op jit(solution)/shard_map/all_gather | solution.py:120
  106.7 93.4 %all-gather.20.cloned.1.call-start = ((), (), s32[]{:S(2)}) async-start(), calls=%async_computation.14 | async-start | bytes 2359296 | tf_op jit(solution)/shard_map/all_gather | solution.py:94
  107.3 253.9 %all-reduce.5.cloned.1.call-start = ((), (), s32[]{:S(2)}) async-start(), calls=%async_computation.15 | async-start | bytes 8388608 | tf_op jit(solution)/shard_map/psum | solution.py:170
  206.1 210.6 %all-gather.22.cloned.1.call-start = ((), (), s32[]{:S(2)}) async-start(), calls=%async_computation.16 | async-start | bytes 9437184 | tf_op jit(solution)/shard_map/all_gather | solution.py:95
  206.8 266.3 %all-gather.24.cloned.1.call-start = ((), (), s32[]{:S(2)}) async-start(), calls=%async_computation.17 | async-start | bytes 9437184 | tf_op jit(solution)/shard_map/all_gather | solution.py:96
  207.6 321.9 %all-gather.26.cloned.1.call-start = ((), (), s32[]{:S(2)}) async-start(), calls=%async_computation.18 | async-start | bytes 9437184 | tf_op jit(solution)/shard_map/all_gather | solution.py:97
  208.2 526.1 %all-reduce.7.cloned.1.call-start = ((), (), s32[]{:S(2)}) async-start(), calls=%async_computation.19 | async-start | bytes 8388608 | tf_op jit(solution)/shard_map/psum | solution.py:203
  579.1 277.8 %reduce-scatter.10.cloned.1.call-start = ((), (), s32[]{:S(2)}) async-start(), calls=%async_computation.20 | async-start | bytes 3145728 | tf_op jit(solution)/shard_map/reduce_scatter | solution.py:248
  826.0 65.7 %reduce-scatter.12.cloned.1.call-start = ((), (), s32[]{:S(2)}) async-start(), calls=%async_computation.21 | async-start | bytes 3145728 | tf_op jit(solution)/shard_map/reduce_scatter | solution.py:251
  826.8 143.2 %reduce-scatter.20.cloned.1.call-start = ((), (), s32[]{:S(2)}) async-start(), calls=%async_computation.25 | async-start | bytes 2359296 | tf_op jit(solution)/shard_map/reduce_scatter | solution.py:289
  834.4 147.1 %reduce-scatter.14.cloned.1.call-start = ((), (), s32[]{:S(2)}) async-start(), calls=%async_computation.22 | async-start | bytes 2359296 | tf_op jit(solution)/shard_map/reduce_scatter | solution.py:280
  874.4 151.5 %reduce-scatter.16.cloned.1.call-start = ((), (), s32[]{:S(2)}) async-start(), calls=%async_computation.23 | async-start | bytes 2359296 | tf_op jit(solution)/shard_map/reduce_scatter | solution.py:283
  881.1 190.1 %reduce-scatter.18.cloned.1.call-start = ((), (), s32[]{:S(2)}) async-start(), calls=%async_computation.24 | async-start | bytes 2359296 | tf_op jit(solution)/shard_map/reduce_scatter | solution.py:286
  897.9 247.8 %reduce-scatter.22.cloned.1.call-start = ((), (), s32[]{:S(2)}) async-start(), calls=%async_computation.26 | async-start | bytes 9437184 | tf_op jit(solution)/shard_map/reduce_scatter | solution.py:292
  912.3 308.6 %reduce-scatter.24.cloned.1.call-start = ((), (), s32[]{:S(2)}) async-start(), calls=%async_computation.27 | async-start | bytes 9437184 | tf_op jit(solution)/shard_map/reduce_scatter | solution.py:295
  926.4 369.1 %reduce-scatter.26.cloned.1.call-start = ((), (), s32[]{:S(2)}) async-start(), calls=%async_computation.28 | async-start | bytes 9437184 | tf_op jit(solution)/shard_map/reduce_scatter | solution.py:298
  940.8 649.7 %all-reduce.9.cloned.1.call-start = ((), (), s32[]{:S(2)}) async-start(), calls=%async_computation.29 | async-start | bytes 16777216 | tf_op jit(solution)/shard_map/psum | solution.py:181
  1073.0 517.5 %copy-start.42 = (f32[1,4,2,128]{3,1,2,0:T(4,128)S(1)}, f32[1,4,2,128]{3,1,2,0:T(4,128)}, u32[]{:S(2)}) copy-start(f32[1,4,2,128]{3,1,2,0:T(4,128)} %copy-done.41) | copy-start | bytes 12292
  1073.0 517.5 %copy-start.44 = (f32[1,4,2,128]{3,1,2,0:T(4,128)S(1)}, f32[1,4,2,128]{3,1,2,0:T(4,128)}, u32[]{:S(2)}) copy-start(f32[1,4,2,128]{3,1,2,0:T(4,128)} %copy-done.43) | copy-start | bytes 12292
  (53 other events, 442.0 us)
Sparse Core Ops, SparseCore 0:
  9.9 30.5 all-gather.17
  42.4 27.8 all-gather.13
  72.2 27.8 all-gather.9
  102.1 33.1 all-gather.15
  137.2 33.1 all-gather.11
  172.1 27.8 all-gather.19
  206.2 154.9 all-reduce.4
  363.3 53.3 all-gather.21
  418.7 54.3 all-gather.23
  475.0 54.3 all-gather.25
  579.3 154.9 all-reduce.6
  826.1 30.8 reduce-scatter.9
  859.9 31.8 reduce-scatter.11
  894.9 41.2 reduce-scatter.19
  940.2 41.2 reduce-scatter.13
  984.6 41.2 reduce-scatter.15
  1029.9 41.2 reduce-scatter.17
  1074.5 71.2 reduce-scatter.21
  1149.6 71.2 reduce-scatter.23
  1224.3 71.2 reduce-scatter.25
  1298.9 291.5 all-reduce.8
where the time goes:
time: 1620 us; the launch traced here: 1610 us
  waiting for transfers between devices  1190 us (73%)
  matrix products  245 us (15%)
  other arithmetic  91.9 us (6%)
  local copies, waits for them, and re-layouts  65.5 us (4%)
  between operations  16.2 us (1%)
    psum x1, waiting for transfers between devices, body(): lax.psum(matmul_trans(hidden_low, full_down).astype(jnp.bfloat16), 'mp')  292 us
    psum x1, waiting for transfers between devices, body(): lax.psum((matmul_trans(grad_gate, full_gate) + matmul_trans(grad_up, full...  155 us
    psum x1, waiting for transfers between devices, body(): lax.psum(matmul_trans(attended_low, full_out).astype(jnp.bfloat16), 'mp')  153 us
    reduce_scatter x1, waiting for transfers between devices, body(): lax.psum_scatter(grad_terms[4].astype(jnp.bfloat16), ('dp', 'seq'), scatt...  72.8 us
    reduce_scatter x1, waiting for transfers between devices, body(): lax.psum_scatter(grad_terms[5].astype(jnp.bfloat16), ('dp', 'seq'), scatt...  72.4 us
    reduce_scatter x1, waiting for transfers between devices, body(): lax.psum_scatter(grad_terms[6].astype(jnp.bfloat16), ('dp', 'seq'), scatt...  71.8 us
    dot_general x7, matrix products, outer_sum(): lax.dot_general(factor_left, factor_right, (((0,), (0,)), ((), ())), pref...  67.9 us
    dot_general x7, matrix products, matmul(): jnp.dot(factor_left, factor_right, preferred_element_type=jnp.float32)  65.3 us
  transfers between devices with their start and end apart: 21, of which 20 were waited for; matrix products, arithmetic and copies ran while one was open for 15% of the time, Pallas kernels for 0%

commit v1 on v0

--- a/solution.py
+++ b/solution.py
@@ -1,8 +1,11 @@
+import functools
 import math
 
 import jax
 import jax.numpy as jnp
 from jax import lax
+from jax.experimental import pallas as pl
+from jax.experimental.pallas import tpu as pltpu
 from jax.sharding import PartitionSpec as P
 
 HD = 128
@@ -62,7 +65,7 @@
     )
 
 
-def body(
+def general_body(
     tokens,
     block_ids,
     query_weight,
@@ -312,6 +315,754 @@
     )
 
 
+MESH = pl.DeviceIdType.MESH
+ANY = pl.BlockSpec(memory_space=pl.ANY)
+VMEM = pl.BlockSpec(memory_space=pltpu.VMEM)
+BF = jnp.bfloat16
+F32 = jnp.float32
+VMEM_LIMIT = 60 * 1024 * 1024
+CHUNK = 64
+BLOCK_ROWS = 256
+TILE = 256
+
+
+def params(collective_id=None):
+    if collective_id is None:
+        return pltpu.CompilerParams(vmem_limit_bytes=VMEM_LIMIT)
+    return pltpu.CompilerParams(
+        collective_id=collective_id, has_side_effects=True, vmem_limit_bytes=VMEM_LIMIT
+    )
+
+
+def dot_nt(left, right):
+    return lax.dot_general(left, right, (((1,), (1,)), ((), ())), preferred_element_type=F32)
+
+
+def dot_tn(left, right):
+    return lax.dot_general(left, right, (((0,), (0,)), ((), ())), preferred_element_type=F32)
+
+
+def dot_nn(left, right):
+    return jnp.dot(left, right, preferred_element_type=F32)
+
+
+def rows_of(index, size):
+    return pl.ds(pl.multiple_of(index * size, size), size)
+
+
+def norm_parts(values):
+    centered = values - jnp.mean(values, axis=-1, keepdims=True)
+    inverse = lax.rsqrt(jnp.mean(centered * centered, axis=-1, keepdims=True) + EPSILON)
+    return centered * inverse, inverse
+
+
+class Tree:
+    def __init__(self, count, acc, from_end, from_mid, out, sems):
+        self.count, self.acc, self.from_end, self.from_mid, self.out = count, acc, from_end, from_mid, out
+        self.sent, self.got_end, self.got_mid, self.fin_sent, self.fin_got, self.fin_kept = sems
+        position = lax.axis_index("mp")
+        self.outer = position + 1 - 2 * (position % 2)
+        self.peer = 3 - position
+        self.is_mid = (position + 1) // 2 == 1
+        self.is_end = (position + 1) // 2 != 1
+
+    def barrier(self, beside_seq=False):
+        barrier = pltpu.get_barrier_semaphore()
+        pl.semaphore_signal(barrier, inc=1, device_id={"mp": self.outer}, device_id_type=MESH)
+
+        @pl.when(self.is_mid)
+        def _():
+            pl.semaphore_signal(barrier, inc=1, device_id={"mp": self.peer}, device_id_type=MESH)
+
+        if beside_seq:
+            other = 1 - lax.axis_index("seq")
+            pl.semaphore_signal(barrier, inc=1, device_id={"seq": other}, device_id_type=MESH)
+        extra = 2 if beside_seq else 1
+        position = lax.axis_index("mp")
+        pl.semaphore_wait(barrier, extra + (position * (3 - position)) // 2)
+
+    def part(self, j):
+        where = rows_of(j, CHUNK)
+        return pltpu.make_async_remote_copy(
+            self.acc.at[where], self.from_end.at[where], self.sent.at[j], self.got_end.at[j],
+            device_id={"mp": self.outer}, device_id_type=MESH,
+        )
+
+    def pair(self, j):
+        where = rows_of(j, CHUNK)
+        return pltpu.make_async_remote_copy(
+            self.acc.at[where], self.from_mid.at[where], self.sent.at[j], self.got_mid.at[j],
+            device_id={"mp": self.peer}, device_id_type=MESH,
+        )
+
+    def final(self, j):
+        where = rows_of(j, CHUNK)
+        return pltpu.make_async_remote_copy(
+            self.from_end.at[where], self.out.at[where], self.fin_sent.at[j], self.fin_got.at[j],
+            device_id={"mp": self.outer}, device_id_type=MESH,
+        )
+
+    def keep(self, j):
+        where = rows_of(j, CHUNK)
+        return pltpu.make_async_copy(self.from_end.at[where], self.out.at[where], self.fin_kept.at[j])
+
+    def send_block(self, block):
+        per_block = BLOCK_ROWS // CHUNK
+
+        @pl.when(self.is_end)
+        def _():
+            for s in range(per_block):
+                self.part(block * per_block + s).start()
+
+    def middle_step(self, i, lag_sum, lag_final, epilogue):
+        j = i - lag_sum
+
+        @pl.when(self.is_mid & (j >= 0) & (j < self.count))
+        def _():
+            self.part(j).wait_recv()
+            where = rows_of(j, CHUNK)
+            self.acc[where] = (self.acc[where].astype(F32) + self.from_end[where].astype(F32)).astype(BF)
+            self.pair(j).start()
+
+        k = i - lag_final
+
+        @pl.when(self.is_mid & (k >= 0) & (k < self.count))
+        def _():
+            self.pair(k).wait_recv()
+            where = rows_of(k, CHUNK)
+            total = self.acc[where].astype(F32) + self.from_mid[where].astype(F32)
+            self.from_end[where] = epilogue(k, total)
+            self.final(k).start()
+            self.keep(k).start()
+
+    def drain(self):
+        @pl.when(self.is_end)
+        def _():
+            def one(j, carry):
+                self.part(j).wait_send()
+                self.final(j).wait_recv()
+                return carry
+
+            lax.fori_loop(0, self.count, one, 0)
+
+        @pl.when(self.is_mid)
+        def _():
+            def one(j, carry):
+                self.pair(j).wait_send()
+                self.final(j).wait_send()
+                self.keep(j).wait()
+                return carry
+
+            lax.fori_loop(0, self.count, one, 0)
+
+
+class Feed:
+    def __init__(self, count, source, slots, sem):
+        self.count, self.source, self.slots, self.sem = count, source, slots, sem
+
+    def copy(self, j):
+        return pltpu.make_async_copy(
+            self.source.at[rows_of(j, CHUNK)], self.slots.at[j % 2], self.sem.at[j % 2]
+        )
+
+    def begin(self):
+        self.copy(0).start()
+        self.copy(1).start()
+
+    def take(self, j):
+        self.copy(j).wait()
+        return self.slots[j % 2]
+
+    def following(self, j):
+        @pl.when(j + 2 < self.count)
+        def _():
+            self.copy(j + 2).start()
+
+
+class Drop:
+    def __init__(self, count, target, slots, sem):
+        self.count, self.target, self.slots, self.sem = count, target, slots, sem
+
+    def copy(self, j):
+        return pltpu.make_async_copy(
+            self.slots.at[j % 2], self.target.at[rows_of(j, CHUNK)], self.sem.at[j % 2]
+        )
+
+    def put(self, j, values):
+        @pl.when(j >= 2)
+        def _():
+            self.copy(j - 2).wait()
+
+        self.slots[j % 2] = values
+        self.copy(j).start()
+
+    def finish(self):
+        self.copy(self.count - 2).wait()
+        self.copy(self.count - 1).wait()
+
+
+def tree_scratch(rows, width):
+    count = rows // CHUNK
+    buffers = [pltpu.VMEM((rows, width), BF) for _ in range(3)]
+    return buffers + [pltpu.SemaphoreType.DMA((count,)) for _ in range(6)]
+
+
+def attention_kernel(q_ref, k_ref, v_ref, ko_ref, vo_ref, qid_ref, kid_ref, koid_ref, o_ref, lse_ref):
+    root = 1.0 / math.sqrt(HD)
+    queries = q_ref[...]
+
+    def scores(keys, ids):
+        raw = dot_nt(keys, queries) * root
+        return jnp.where(ids <= qid_ref[0], raw, MASKED)
+
+    own = scores(k_ref[...], kid_ref[0])
+    other = scores(ko_ref[...], koid_ref[0])
+    top = jnp.maximum(jnp.max(own, axis=0, keepdims=True), jnp.max(other, axis=0, keepdims=True))
+    own, other = jnp.exp(own - top), jnp.exp(other - top)
+    total = jnp.sum(own, axis=0, keepdims=True) + jnp.sum(other, axis=0, keepdims=True)
+    scale = 1.0 / total
+    mixed = dot_tn(v_ref[...], (own * scale).astype(BF)) + dot_tn(vo_ref[...], (other * scale).astype(BF))
+    o_ref[...] = mixed.T.astype(BF)
+    lse_ref[0] = top + jnp.log(total)
+
+
+def attention(queries, kv_own, kv_other, qid, kid, koid, groups, shard_len):
+    rows, width = queries.shape
+    heads = width // HD
+    tile = lambda shift: pl.BlockSpec((shard_len, HD), lambda g, h: (g, h + shift))
+    row = pl.BlockSpec((1, 1, shard_len), lambda g, h: (g, 0, 0))
+    column = pl.BlockSpec((1, shard_len, 1), lambda g, h: (g, 0, 0))
+    return pl.pallas_call(
+        attention_kernel,
+        grid=(groups, heads),
+        out_shape=(
+            jax.ShapeDtypeStruct((rows, width), BF),
+            jax.ShapeDtypeStruct((groups * heads, 1, shard_len), F32),
+        ),
+        in_specs=[tile(0), tile(0), tile(heads), tile(0), tile(heads), row, column, column],
+        out_specs=(tile(0), pl.BlockSpec((1, 1, shard_len), lambda g, h: (g * heads + h, 0, 0))),
+        compiler_params=params(),
+    )(queries, kv_own, kv_own, kv_other, kv_other, qid, kid, koid)
+
+
+def branch_kernel(count, att_ref, w_ref, tok_ref, n2_ref, mid_ref, acc, from_end, from_mid, *rest):
+    sems, (mid_slots, mid_sem) = rest[:6], rest[6:]
+    tree = Tree(count, acc, from_end, from_mid, n2_ref, sems)
+    drop = Drop(count, mid_ref, mid_slots, mid_sem)
+    tree.barrier()
+    per_block = BLOCK_ROWS // CHUNK
+
+    def epilogue(j, total):
+        middle = tok_ref[rows_of(j, CHUNK)].astype(F32) + total
+        drop.put(j, middle)
+        return norm_parts(middle)[0].astype(BF)
+
+    def step(i, carry):
+        @pl.when((i % per_block == 0) & (i < count))
+        def _():
+            block = i // per_block
+            where = rows_of(block, BLOCK_ROWS)
+            acc[where] = dot_nt(att_ref[where], w_ref[...]).astype(BF)
+            tree.send_block(block)
+
+        tree.middle_step(i, 1, 3, epilogue)
+        return carry
+
+    lax.fori_loop(0, count + 3, step, 0)
+    tree.drain()
+
+    @pl.when(tree.is_mid)
+    def _():
+        drop.finish()
+
+
+def branch_sum(attended, merged, tokens):
+    rows, width = attended.shape
+    model = tokens.shape[1]
+    count = rows // CHUNK
+    return pl.pallas_call(
+        functools.partial(branch_kernel, count),
+        grid=(1,),
+        out_shape=(jax.ShapeDtypeStruct((rows, model), BF), jax.ShapeDtypeStruct((rows, model), F32)),
+        in_specs=[VMEM, pl.BlockSpec((model, width), lambda _: (0, 3)), VMEM],
+        out_specs=(ANY, ANY),
+        scratch_shapes=tree_scratch(rows, model)
+        + [pltpu.VMEM((2, CHUNK, model), F32), pltpu.SemaphoreType.DMA((2,))],
+        compiler_params=params(1),
+    )(attended, merged, tokens)
+
+
+def feed_kernel(
+    count, n2_ref, og_ref, wf_ref, mid_ref, gb_ref, gm_ref, hid_ref, ggu_ref,
+    acc, from_end, from_mid, *rest,
+):
+    sems, rest = rest[:6], rest[6:]
+    wg, wu, wd, w_sem, xs, ogs, in_sem, hs, gs, us, out_sem, mid_slots, mid_sem, og_slots, og_sem, gm_slots, gm_sem = rest
+    tree = Tree(count, acc, from_end, from_mid, gb_ref, sems)
+    mid_feed = Feed(count, mid_ref, mid_slots, mid_sem)
+    og_feed = Feed(count, og_ref, og_slots, og_sem)
+    drop = Drop(count, gm_ref, gm_slots, gm_sem)
+    hidden = wg.shape[1]
+    per_block = BLOCK_ROWS // CHUNK
+    blocks = count // per_block
+
+    def weight(k, target):
+        return pltpu.make_async_copy(wf_ref.at[:, pl.ds(k * hidden, hidden)], target, w_sem.at[k])
+
+    def load(block):
+        where, slot = rows_of(block, BLOCK_ROWS), block % 2
+        return (
+            pltpu.make_async_copy(n2_ref.at[where], xs.at[slot], in_sem.at[0, slot]),
+            pltpu.make_async_copy(og_ref.at[where], ogs.at[slot], in_sem.at[1, slot]),
+        )
+
+    def store(block):
+        where = rows_of(block, BLOCK_ROWS)
+        return (
+            pltpu.make_async_copy(hs, hid_ref.at[where], out_sem.at[0]),
+            pltpu.make_async_copy(gs, ggu_ref.at[where, pl.ds(0, hidden)], out_sem.at[1]),
+            pltpu.make_async_copy(us, ggu_ref.at[where, pl.ds(hidden, hidden)], out_sem.at[2]),
+        )
+
+    for block in range(2):
+        for copy in load(block):
+            copy.start()
+    for k, target in enumerate((wg, wu, wd)):
+        weight(k, target).start()
+
+    @pl.when(tree.is_mid)
+    def _():
+        mid_feed.begin()
+        og_feed.begin()
+
+    tree.barrier()
+    for k, target in enumerate((wg, wu, wd)):
+        weight(k, target).wait()
+
+    def epilogue(j, total):
+        normed, inverse = norm_parts(mid_feed.take(j))
+        og = og_feed.take(j).astype(F32)
+        spread = total - jnp.mean(total, axis=-1, keepdims=True)
+        grad = og + inverse * (spread - normed * jnp.mean(total * normed, axis=-1, keepdims=True))
+        mid_feed.following(j)
+        og_feed.following(j)
+        drop.put(j, grad)
+        return grad.astype(BF)
+
+    def step(i, carry):
+        block, quarter = i // per_block, i % per_block
+        slot = block % 2
+
+        @pl.when((i < count) & (quarter == 0))
+        def _():
+            for copy in load(block):
+                copy.wait()
+
+            @pl.when(block >= 1)
+            def _():
+                for copy in store(block - 1):
+                    copy.wait()
+
+        half = per_block // 2
+        tiles = hidden // TILE // half
+
+        @pl.when((i < count) & (quarter < half))
+        def _():
+            def tile(t, carry):
+                at = pl.ds(pl.multiple_of((quarter * tiles + t) * TILE, TILE), TILE)
+                gate = dot_nn(xs[slot], wg[:, at])
+                up = dot_nn(xs[slot], wu[:, at])
+                back = dot_nn(ogs[slot], wd[:, at])
+                sig = jax.nn.sigmoid(gate)
+                act = gate * sig
+                hs[:, at] = (act * up).astype(BF)
+                gs[:, at] = (back * up * sig * (1.0 + gate * (1.0 - sig))).astype(BF)
+                us[:, at] = (back * act).astype(BF)
+                return carry
+
+            lax.fori_loop(0, tiles, tile, 0)
+
+        @pl.when((i < count) & (quarter >= half))
+        def _():
+            where = rows_of(block, BLOCK_ROWS)
+            tiles_out = acc.shape[1] // TILE // half
+
+            def tile(t, carry):
+                at = pl.ds(pl.multiple_of(((quarter - half) * tiles_out + t) * TILE, TILE), TILE)
+                acc[where, at] = (dot_nt(gs[...], wg[at, :]) + dot_nt(us[...], wu[at, :])).astype(BF)
+                return carry
+
+            lax.fori_loop(0, tiles_out, tile, 0)
+
+        @pl.when((i < count) & (quarter == per_block - 1))
+        def _():
+            for copy in store(block):
+                copy.start()
+
+            @pl.when(block + 2 < blocks)
+            def _():
+                for copy in load(block + 2):
+                    copy.start()
+
+            tree.send_block(block)
+
+        tree.middle_step(i, per_block + 1, per_block + 3, epilogue)
+        return carry
+
+    lax.fori_loop(0, count + per_block + 3, step, 0)
+    for copy in store(blocks - 1):
+        copy.wait()
+    tree.drain()
+
+    @pl.when(tree.is_mid)
+    def _():
+        drop.finish()
+
+
+def feed_forward(normed_two, out_grad, merged, middle):
+    rows, model = normed_two.shape
+    hidden = merged.shape[1] // 3
+    count = rows // CHUNK
+    block = lambda *lead: pltpu.VMEM((*lead, BLOCK_ROWS, model), BF)
+    tall = lambda: pltpu.VMEM((model, hidden), BF)
+    wide = lambda kind: [pltpu.VMEM((2, CHUNK, model), kind), pltpu.SemaphoreType.DMA((2,))]
+    return pl.pallas_call(
+        functools.partial(feed_kernel, count),
+        out_shape=(
+            jax.ShapeDtypeStruct((rows, model), BF),
+            jax.ShapeDtypeStruct((rows, model), F32),
+            jax.ShapeDtypeStruct((rows, hidden), BF),
+            jax.ShapeDtypeStruct((rows, 2 * hidden), BF),
+        ),
+        in_specs=[ANY] * 4,
+        out_specs=(ANY,) * 4,
+        scratch_shapes=tree_scratch(rows, model)
+        + [tall(), tall(), tall(), pltpu.SemaphoreType.DMA((3,))]
+        + [block(2), block(2), pltpu.SemaphoreType.DMA((2, 2))]
+        + [pltpu.VMEM((BLOCK_ROWS, hidden), BF) for _ in range(3)]
+        + [pltpu.SemaphoreType.DMA((3,))]
+        + wide(F32) + wide(BF) + wide(F32),
+        compiler_params=params(2),
+    )(normed_two, out_grad, merged, middle)
+
+
+def back_kernel(
+    count, groups, heads,
+    hid_ref, wf_ref, mid_ref, gb_ref, wo_ref, q_ref, kv_ref, kvo_ref, lse_ref,
+    qid_ref, kid_ref, koid_ref, cos_ref, sin_ref,
+    out_ref, dqkv_ref,
+    acc, from_end, from_mid, *rest,
+):
+    sems, rest = rest[:6], rest[6:]
+    wd, wd_sem, hs, hs_sem, gbs, gbs_sem, mid_slots, mid_sem, ga, probs, gprobs, dkv, dkv_out, dkv_in, dkv_sent, dkv_got = rest
+    tree = Tree(count, acc, from_end, from_mid, out_ref, sems)
+    mid_feed = Feed(count, mid_ref, mid_slots, mid_sem)
+    per_block = BLOCK_ROWS // CHUNK
+    blocks = count // per_block
+    hidden = wd.shape[1]
+    shard_len = q_ref.shape[0] // groups
+    width = heads * HD
+    root = 1.0 / math.sqrt(HD)
+    other = 1 - lax.axis_index("seq")
+
+    def load_hidden(block):
+        return pltpu.make_async_copy(
+            hid_ref.at[rows_of(block, BLOCK_ROWS)], hs.at[block % 2], hs_sem.at[block % 2]
+        )
+
+    def load_branch(block):
+        return pltpu.make_async_copy(
+            gb_ref.at[rows_of(block, BLOCK_ROWS)], gbs.at[block % 2], gbs_sem.at[block % 2]
+        )
+
+    def cross(p):
+        return pltpu.make_async_remote_copy(
+            dkv_out.at[p], dkv_in.at[p], dkv_sent.at[p], dkv_got.at[p],
+            device_id={"seq": other}, device_id_type=MESH,
+        )
+
+    weight = pltpu.make_async_copy(wf_ref.at[:, pl.ds(2 * hidden, hidden)], wd, wd_sem.at[0])
+    weight.start()
+    for block in range(2):
+        load_hidden(block).start()
+        load_branch(block).start()
+
+    @pl.when(tree.is_mid)
+    def _():
+        mid_feed.begin()
+
+    tree.barrier(beside_seq=True)
+    weight.wait()
+
+    def epilogue(j, total):
+        result = (mid_feed.take(j) + total).astype(BF)
+        mid_feed.following(j)
+        return result
+
+    def pair_back(p):
+        group, head = p // heads, p % heads
+        where = rows_of(group, shard_len)
+        lane = lambda shift: pl.ds(pl.multiple_of((head + shift) * HD, HD), HD)
+        queries, grads = q_ref[where, lane(0)], ga[where, lane(0)]
+        delta = jnp.zeros((1, shard_len), F32)
+        sources = ((kv_ref, kid_ref), (kvo_ref, koid_ref))
+        for s, (source, ids) in enumerate(sources):
+            at = pl.ds(s * shard_len, shard_len)
+            raw = dot_nt(source[where, lane(0)], queries) * root
+            prob = jnp.where(ids[group] <= qid_ref[group], jnp.exp(raw - lse_ref[p]), 0.0)
+            gprob = dot_nt(source[where, lane(heads)], grads)
+            delta = delta + jnp.sum(prob * gprob, axis=0, keepdims=True)
+            probs[at] = prob
+            gprobs[at] = gprob
+        turned = jnp.zeros((HD, shard_len), F32)
+        for s, (source, ids) in reversed(list(enumerate(sources))):
+            at = pl.ds(s * shard_len, shard_len)
+            prob = probs[at]
+            graw = (prob * (gprobs[at] - delta) * root).astype(BF)
+            gkeys = dot_nn(graw, queries)
+            gvalues = dot_nn(prob.astype(BF), grads)
+            if s == 1:
+                dkv_out[p, :, pl.ds(0, HD)] = gkeys.astype(BF)
+                dkv_out[p, :, pl.ds(HD, HD)] = gvalues.astype(BF)
+                cross(p).start()
+            else:
+                dkv[p, :, pl.ds(0, HD)] = gkeys
+                dkv[p, :, pl.ds(HD, HD)] = gvalues
+            turned = turned + dot_tn(source[where, lane(0)], graw)
+        dqkv_ref[where, lane(0)] = turn_back(turned.T).astype(BF)
+
+    def turn_back(values):
+        return values * cos_ref[...] + pltpu.roll(values, HD // 2, 1) * sin_ref[...]
+
+    def step(i, carry):
+        @pl.when((i % per_block == 0) & (i < count))
+        def _():
+            block = i // per_block
+            where = rows_of(block, BLOCK_ROWS)
+            load_hidden(block).wait()
+            tiles = acc.shape[1] // (2 * TILE)
+
+            def tile(t, carry):
+                at = pl.ds(pl.multiple_of(t * 2 * TILE, 2 * TILE), 2 * TILE)
+                acc[where, at] = dot_nt(hs[block % 2], wd[at, :]).astype(BF)
+                return carry
+
+            lax.fori_loop(0, tiles, tile, 0)
+            tree.send_block(block)
+
+            @pl.when(block + 2 < blocks)
+            def _():
+                load_hidden(block + 2).start()
+
+        @pl.when(i == 1)
+        def _():
+            for block in range(blocks):
+                load_branch(block).wait()
+                ga[rows_of(block, BLOCK_ROWS)] = dot_nn(gbs[block % 2], wo_ref[...]).astype(BF)
+                if block + 2 < blocks:
+                    load_branch(block + 2).start()
+
+        @pl.when((i >= 2) & (i < 2 + groups * heads))
+        def _():
+            pair_back(i - 2)
+
+        tree.middle_step(i, 1, 3, epilogue)
+        return carry
+
+    lax.fori_loop(0, count + 3, step, 0)
+
+    def gather(p, carry):
+        group, head = p // heads, p % heads
+        where = rows_of(group, shard_len)
+        lane = lambda shift: pl.ds(pl.multiple_of((head + shift) * HD, HD), HD)
+        cross(p).wait_recv()
+        gkeys = dkv[p, :, pl.ds(0, HD)] + dkv_in[p, :, pl.ds(0, HD)].astype(F32)
+        gvalues = dkv[p, :, pl.ds(HD, HD)] + dkv_in[p, :, pl.ds(HD, HD)].astype(F32)
+        dqkv_ref[where, lane(heads)] = turn_back(gkeys).astype(BF)
+        dqkv_ref[where, lane(2 * heads)] = gvalues.astype(BF)
+        cross(p).wait_send()
+        return carry
+
+    lax.fori_loop(0, groups * heads, gather, 0)
+    tree.drain()
+
+
+def feed_sum_and_attention_back(
+    hidden_low, merged_feed, middle, grad_branch, merged, queries, kv_own, kv_other, lse,
+    qid, kid, koid, cosine, sine_back, groups,
+):
+    rows, hidden = hidden_low.shape
+    model, width = middle.shape[1], queries.shape[1]
+    heads = width // HD
+    count = rows // CHUNK
+    shard_len = rows // groups
+    pairs = groups * heads
+    sem = lambda *shape: pltpu.SemaphoreType.DMA(shape)
+    return pl.pallas_call(
+        functools.partial(back_kernel, count, groups, heads),
+        grid=(1,),
+        out_shape=(jax.ShapeDtypeStruct((rows, model), BF), jax.ShapeDtypeStruct((rows, 3 * width), BF)),
+        in_specs=[ANY] * 4
+        + [pl.BlockSpec((model, width), lambda _: (0, 3))]
+        + [VMEM] * 9,
+        out_specs=(ANY, VMEM),
+        scratch_shapes=tree_scratch(rows, model)
+        + [
+            pltpu.VMEM((model, hidden), BF), sem(1),
+            pltpu.VMEM((2, BLOCK_ROWS, hidden), BF), sem(2),
+            pltpu.VMEM((2, BLOCK_ROWS, model), BF), sem(2),
+            pltpu.VMEM((2, CHUNK, model), F32), sem(2),
+            pltpu.VMEM((rows, width), BF),
+            pltpu.VMEM((2 * shard_len, shard_len), F32),
+            pltpu.VMEM((2 * shard_len, shard_len), F32),
+            pltpu.VMEM((pairs, shard_len, 2 * HD), F32),
+            pltpu.VMEM((pairs, shard_len, 2 * HD), BF),
+            pltpu.VMEM((pairs, shard_len, 2 * HD), BF),
+            sem(pairs), sem(pairs),
+        ],
+        compiler_params=params(3),
+    )(
+        hidden_low, merged_feed, middle, grad_branch, merged, queries, kv_own, kv_other, lse,
+        qid, kid, koid, cosine, sine_back,
+    )
+
+
+def first_kernel(count, dqkv_ref, w_ref, tok_ref, gm_ref, out_ref, acc, from_end, from_mid, *rest):
+    sems, (gm_slots, gm_sem) = rest[:6], rest[6:]
+    tree = Tree(count, acc, from_end, from_mid, out_ref, sems)
+    feed = Feed(count, gm_ref, gm_slots, gm_sem)
+    per_block = BLOCK_ROWS // CHUNK
+
+    @pl.when(tree.is_mid)
+    def _():
+        feed.begin()
+
+    tree.barrier()
+
+    def epilogue(j, total):
+        normed, inverse = norm_parts(tok_ref[rows_of(j, CHUNK)].astype(F32))
+        spread = total - jnp.mean(total, axis=-1, keepdims=True)
+        grad = inverse * (spread - normed * jnp.mean(total * normed, axis=-1, keepdims=True))
+        result = (feed.take(j) + grad).astype(BF)
+        feed.following(j)
+        return result
+
+    def step(i, carry):
+        @pl.when((i % per_block == 0) & (i < count))
+        def _():
+            block = i // per_block
+            where = rows_of(block, BLOCK_ROWS)
+            acc[where] = dot_nt(dqkv_ref[where], w_ref[...]).astype(BF)
+            tree.send_block(block)
+
+        tree.middle_step(i, 1, 3, epilogue)
+        return carry
+
+    lax.fori_loop(0, count + 3, step, 0)
+    tree.drain()
+
+
+def first_sum(dqkv, merged, tokens, grad_middle):
+    rows, width = dqkv.shape
+    model = tokens.shape[1]
+    count = rows // CHUNK
+    return pl.pallas_call(
+        functools.partial(first_kernel, count),
+        grid=(1,),
+        out_shape=jax.ShapeDtypeStruct((rows, model), BF),
+        in_specs=[VMEM, pl.BlockSpec((model, width), lambda _: (0, 0)), VMEM, ANY],
+        out_specs=ANY,
+        scratch_shapes=tree_scratch(rows, model)
+        + [pltpu.VMEM((2, CHUNK, model), F32), pltpu.SemaphoreType.DMA((2,))],
+        compiler_params=params(4),
+    )(dqkv, merged, tokens, grad_middle)
+
+
+def gathered(shard):
+    return lax.all_gather(shard, ("dp", "seq"), axis=0, tiled=True)
+
+
+def scattered(term):
+    return lax.psum_scatter(term, ("dp", "seq"), scatter_dimension=0, tiled=True).astype(F32)
+
+
+def tree_body(
+    tokens,
+    block_ids,
+    query_weight,
+    key_weight,
+    value_weight,
+    out_weight,
+    gate_weight,
+    up_weight,
+    down_weight,
+    out_grad,
+):
+    groups, shard_len, model = tokens.shape
+    rows = groups * shard_len
+    seq_rank = lax.axis_index("seq")
+    merged = gathered(jnp.concatenate([query_weight, key_weight, value_weight, out_weight], axis=1))
+    width = query_weight.shape[1]
+    heads = width // HD
+    feed_shard = jnp.concatenate([gate_weight, up_weight, down_weight], axis=1)
+    feed_shard, merged = lax.optimization_barrier((feed_shard, merged))
+    merged_feed = gathered(feed_shard)
+
+    positions = (seq_rank * shard_len + jnp.arange(shard_len)).astype(F32)
+    cosine, sine = rope_tables(positions)
+    sign = jnp.concatenate([jnp.ones((HD // 2,), F32), -jnp.ones((HD // 2,), F32)])
+    sine_back = sine * sign
+    flat_tokens = tokens.reshape(rows, model)
+    normed_low = layer_norm(flat_tokens.astype(F32))[0].astype(BF)
+
+    shape_heads = (groups, shard_len, heads, HD)
+    lin_k = matmul(normed_low, merged[:, width : 2 * width]).reshape(shape_heads)
+    keys = rotate(lin_k, cosine[None, :, None, :], sine[None, :, None, :]).astype(BF).reshape(rows, width)
+    values = matmul(normed_low, merged[:, 2 * width : 3 * width]).astype(BF)
+    kv_own = jnp.concatenate([keys, values], axis=1)
+    kv_other = lax.ppermute(kv_own, "seq", [(0, 1), (1, 0)])
+    lin_q = matmul(normed_low, merged[:, :width]).reshape(shape_heads)
+    queries = rotate(lin_q, cosine[None, :, None, :], sine[None, :, None, :]).astype(BF).reshape(rows, width)
+
+    own_ids = lax.dynamic_slice_in_dim(block_ids, seq_rank * shard_len, shard_len, 1)
+    other_ids = lax.dynamic_slice_in_dim(block_ids, (1 - seq_rank) * shard_len, shard_len, 1)
+    qid, kid, koid = own_ids[:, None, :], own_ids[:, :, None], other_ids[:, :, None]
+
+    attended, lse = attention(queries, kv_own, kv_other, qid, kid, koid, groups, shard_len)
+    normed_two, middle = branch_sum(attended, merged, flat_tokens)
+    grad_low = out_grad.reshape(rows, model)
+    grad_branch, grad_middle, hidden_low, grad_gate_up = feed_forward(
+        normed_two, grad_low, merged_feed, middle
+    )
+    feed_terms = jnp.concatenate(
+        [outer_sum(normed_two, grad_gate_up).astype(BF), outer_sum(grad_low, hidden_low).astype(BF)], axis=1
+    )
+    hidden_low, feed_terms = lax.optimization_barrier((hidden_low, feed_terms))
+    feed_grads = scattered(feed_terms)
+    output, dqkv = feed_sum_and_attention_back(
+        hidden_low, merged_feed, middle, grad_branch, merged, queries, kv_own, kv_other, lse,
+        qid, kid, koid, cosine, sine_back, groups,
+    )
+    head_terms = jnp.concatenate(
+        [outer_sum(normed_low, dqkv).astype(BF), outer_sum(grad_branch, attended).astype(BF)], axis=1
+    )
+    dqkv, head_terms = lax.optimization_barrier((dqkv, head_terms))
+    head_grads = scattered(head_terms)
+    tokens_grad = first_sum(dqkv, merged, flat_tokens, grad_middle)
+    hidden = gate_weight.shape[1]
+    return (
+        output.reshape(tokens.shape),
+        tokens_grad.reshape(tokens.shape),
+        head_grads[:, :width],
+        head_grads[:, width : 2 * width],
+        head_grads[:, 2 * width : 3 * width],
+        head_grads[:, 3 * width :],
+        feed_grads[:, :hidden],
+        feed_grads[:, hidden : 2 * hidden],
+        feed_grads[:, 2 * hidden :],
+    )
+
+
 def solution(mesh):
     in_specs = (
         P("dp", "seq", None),
@@ -336,4 +1087,6 @@
         P(("dp", "seq"), "mp"),
         P(("dp", "seq"), "mp"),
     )
+    fits = mesh.shape["seq"] == 2 and mesh.shape["mp"] == 4
+    body = tree_body if fits else general_body
     return jax.shard_map(body, mesh=mesh, in_specs=in_specs, out_specs=out_specs, check_vma=False)

time: 1620 us -> 910 us (0.56)
  waiting for transfers between devices: 1190 us -> 243 us
  Pallas kernels: 0 us -> 503 us
  matrix products: 245 us -> 67.7 us
  other arithmetic: 91.9 us -> 43.6 us
  local copies, waits for them, and re-layouts: 65.5 us -> 33.9 us
    psum x3 -> x0, waiting for transfers between devices: 600 us -> none  [the longest x1 292 us: body(): lax.psum(matmul_trans(hidden_low, full_down).astype(jnp.bfloat16), 'mp')]
    pallas_call x0 -> x5, Pallas kernels: none -> 503 us  [the longest x1 135 us: feed_forward(): pl.pallas_call(functools.partial(feed_kernel, count), out_shape=(jax.Shap...]
    reduce_scatter x9 -> x2, waiting for transfers between devices: 346 us -> 109 us  [scattered(): lax.psum_scatter(term, ('dp', 'seq'), scatter_dimension=0, tiled=True)]
    all_gather x9 -> x2, waiting for transfers between devices: 242 us -> 54.8 us  [gathered(): return lax.all_gather(shard, ('dp', 'seq'), axis=0, tiled=True)]
    dot_general x21 -> x0, matrix products: 112 us -> none  [the longest x7 58.7 us: matmul_trans(): lax.dot_general(factor_left, factor_right, (((1,), (1,)), ((), ())), pref...]
    ppermute x0 -> x1, waiting for transfers between devices: none -> 78.6 us  [tree_body(): kv_other = lax.ppermute(kv_own, 'seq', [(0, 1), (1, 0)])]
    dot_general x7 -> x3, matrix products: 65.3 us -> 13.3 us  [matmul(): jnp.dot(factor_left, factor_right, preferred_element_type=jnp.float32)]
    convert_element_type x15 -> x3, other arithmetic: 41.9 us -> 5.68 us  [the longest x1 3.5 us: tree_body(): normed_low = layer_norm(flat_tokens.astype(F32))[0].astype(BF)]
  transfers between devices with their start and end apart: 21 -> 5, of which waited for: 20 -> 3; matrix products, arithmetic and copies ran while one was open for 15% -> 5% of each run, Pallas kernels for 0% -> 27%
where the time goes in v1:
time: 910 us; the launch traced here: 906 us
  Pallas kernels  503 us (55%)
  waiting for transfers between devices  243 us (27%)
  matrix products  67.7 us (7%)
  other arithmetic  43.6 us (5%)
  local copies, waits for them, and re-layouts  33.9 us (4%)
  between operations  14.3 us (2%)
    pallas_call x1, Pallas kernels, feed_forward(): pl.pallas_call(functools.partial(feed_kernel, count), out_shape=(jax.Shap...  135 us
    pallas_call x1, Pallas kernels, feed_sum_and_attention_back(): pl.pallas_call(functools.partial(back_kernel, count, groups, heads), grid...  123 us
    pallas_call x1, Pallas kernels, first_sum(): pl.pallas_call(functools.partial(first_kernel, count), grid=(1,), out_sha...  117 us
    pallas_call x1, Pallas kernels, branch_sum(): pl.pallas_call(functools.partial(branch_kernel, count), grid=(1,), out_sh...  117 us
    reduce_scatter x2, waiting for transfers between devices, scattered(): lax.psum_scatter(term, ('dp', 'seq'), scatter_dimension=0, tiled=True)  109 us
    ppermute x1, waiting for transfers between devices, tree_body(): kv_other = lax.ppermute(kv_own, 'seq', [(0, 1), (1, 0)])  78.6 us
    all_gather x2, waiting for transfers between devices, gathered(): return lax.all_gather(shard, ('dp', 'seq'), axis=0, tiled=True)  54.8 us
    dot_general x4, matrix products, outer_sum(): lax.dot_general(factor_left, factor_right, (((0,), (0,)), ((), ())), pref...  54.4 us
  transfers between devices with their start and end apart: 5, of which 3 were waited for; matrix products, arithmetic and copies ran while one was open for 5% of the time, Pallas kernels for 27%

profile of v1, /device:TPU:0, one launch (start us, length us, event | category | flops | bytes accessed | tf_op | source)
XLA Modules:
  0.0 906.4 jit_solution(2504264312955327991)
XLA Ops:
  9.6 3.2 pad_maximum_fusion.2
  12.8 54.8 %all-gather.3.cloned.1.call-done.w_ref.wo_ref = bf16[2048,2048]{1,0:T(8,128)(2,1)} async-done(((bf16[256,2048]{1,0:T(8,128)(2,1)}), bf16[2048,2048]{1,0:T(8,128)(2,1)}) %all-gather.3.cloned.1.call-update) | async-done | bytes 8388624 | tf_op jit(solution)/shard_map/all_gather | solution.py:982
  70.0 3.0 convert_reduce_fusion
  74.7 3.5 multiply_convert_fusion
  78.2 2.3 copy-done.2
  82.2 4.1 copy.50
  86.3 2.4 copy.51
  88.7 5.5 fusion.7
  94.3 2.6 fusion.5
  100.8 5.2 fusion.15
  112.6 78.6 %collective-permute-done.ko_ref.vo_ref.kvo_ref = bf16[1024,1024]{1,0:T(8,128)(2,1)} collective-permute-done((bf16[1024,1024]{1,0:T(8,128)(2,1)S(1)}, bf16[1024,1024]{1,0:T(8,128)(2,1)}, u32[]{:S(2)}, u32[]{:S(2)}) %collective-permute-start) | collective-permute-done | bytes 2097184 | tf_op jit(solution)/shard_map/ppermute | solution.py:1023
  191.2 12.6 %shard_map.169 = (bf16[1024,512]{1,0:T(8,128)(2,1)}, f32[8,1,512]{2,1,0:T(1,128)}) custom-call(bf16[1024,512]{1,0:T(8,128)(2,1)} %bitcast.56, bf16[1024,1024]{1,0:T(8,128)(2,1)} %copy-done.3, bf16[1024,1024]{1,0:T(8,128)(2,1)} %copy-done.3, bf16[1024,1024]{1,0:T(8,128)(2,1)} %collective-permute-done.ko_ref.vo_ref.kvo_ref, ...), custom_call_target="tpu_custom_call" | custom-call | tf_op jit(solution)/shard_map/pallas_call | solution.py:535
  203.8 116.5 %shard_map.170 = (bf16[1024,2048]{1,0:T(8,128)(2,1)}, f32[1024,2048]{1,0:T(8,128)}) custom-call(bf16[1024,512]{1,0:T(8,128)(2,1)} %get-tuple-element.26.att_ref, bf16[2048,2048]{1,0:T(8,128)(2,1)} %all-gather.3.cloned.1.call-done.w_ref.wo_ref, bf16[1024,2048]{1,0:T(8,128)(2,1)} %bitcast.53), custom_call_target="tpu_custom_call" | custom-call | tf_op jit(solution)/shard_map/pallas_call | solution.py:583
  320.4 134.9 %shard_map.171 = (bf16[1024,2048]{1,0:T(8,128)(2,1)}, f32[1024,2048]{1,0:T(8,128)}, bf16[1024,2048]{1,0:T(8,128)(2,1)}, bf16[1024,4096]{1,0:T(8,128)(2,1)}) custom-call(bf16[1024,2048]{1,0:T(8,128)(2,1)} %get-tuple-element.27.n2_ref, bf16[1024,2048]{1,0:T(8,128)(2,1)} %bitcast.58, bf16[2048,6144]{1,0:T(8,128)(2,1)} %all-gather.5.cloned.1.call-done.wf_ref, ...), custom_call_target="tpu_custom_call" | custom-call | tf_op jit(solution)/shard_map/pallas_call | solution.py:729
  455.3 24.7 %convolution_convert_fusion = bf16[2048,4096]{1,0:T(8,128)(2,1)} fusion(bf16[1024,2048]{1,0:T(8,128)(2,1)} %get-tuple-element.27.n2_ref, bf16[1024,4096]{1,0:T(8,128)(2,1)} %get-tuple-element.31), kind=kOutput, calls=%fused_computation.1 | convolution fusion | flops 17188257792 | bytes 29360128 | tf_op jit(solution)/shard_map/dot_general | solution.py:63
  480.1 13.5 %convert_bitcast_fusion = bf16[2048,2048]{1,0:T(8,128)(2,1)} fusion(bf16[1024,2048]{1,0:T(8,128)(2,1)} %get-tuple-element.32.hid_ref, bf16[1024,2048]{1,0:T(8,128)(2,1)S(1)} %bitcast.59), kind=kOutput, calls=%fused_computation.9 | convolution fusion | flops 8594128896 | bytes 16777216 | tf_op jit(solution)/shard_map/dot_general | solution.py:63
  493.6 17.7 %pad_maximum_fusion = bf16[2048,6144]{1,0:T(8,128)(2,1)} fusion(bf16[2048,2048]{1,0:T(8,128)(2,1)} %convert_bitcast_fusion, bf16[2048,4096]{1,0:T(8,128)(2,1)} %convolution_convert_fusion), kind=kLoop, calls=%fused_computation | loop fusion | flops 50331648 | bytes 50331648 | tf_op jit(solution)/shard_map/concatenate | solution.py:1037
  511.3 4.6 convolution_convert_fusion.2
  515.8 122.7 %shard_map.172 = (bf16[1024,2048]{1,0:T(8,128)(2,1)}, bf16[1024,1536]{1,0:T(8,128)(2,1)}) custom-call(bf16[1024,2048]{1,0:T(8,128)(2,1)} %get-tuple-element.32.hid_ref, bf16[2048,6144]{1,0:T(8,128)(2,1)} %all-gather.5.cloned.1.call-done.wf_ref, f32[1024,2048]{1,0:T(8,128)} %get-tuple-element.29.mid_ref, bf16[1024,2048]{1,0:T(8,128)(2,1)} %get-tuple-element.33.gb_ref, ...), custom_call_target="tpu_custom_call" | custom-call | tf_op jit(solution)/shard_map/pallas_call | solution.py:901
  638.5 11.5 %convolution_convert_fusion.1 = bf16[2048,1536]{0,1:T(8,128)(2,1)} fusion(bf16[1024,2048]{1,0:T(8,128)(2,1)} %multiply_convert_fusion, bf16[1024,1536]{1,0:T(8,128)(2,1)} %get-tuple-element.37.dqkv_ref), kind=kOutput, calls=%fused_computation.11 | convolution fusion | flops 6445596672 | bytes 13631488 | tf_op jit(solution)/shard_map/dot_general | solution.py:63
  650.0 7.6 pad_maximum_fusion.1
  658.3 116.5 %shard_map.173 = bf16[1024,2048]{1,0:T(8,128)(2,1)} custom-call(bf16[1024,1536]{1,0:T(8,128)(2,1)} %get-tuple-element.37.dqkv_ref, bf16[2048,2048]{1,0:T(8,128)(2,1)} %all-gather.3.cloned.1.call-done.w_ref.wo_ref, bf16[1024,2048]{1,0:T(8,128)(2,1)} %bitcast.54, f32[1024,2048]{1,0:T(8,128)} %get-tuple-element.38.gm_ref), custom_call_target="tpu_custom_call" | custom-call | tf_op jit(solution)/shard_map/pallas_call | solution.py:969
  780.4 108.6 %reduce-scatter.5.cloned.1.call-done = bf16[256,6144]{1,0:T(8,128)(2,1)} async-done(((bf16[2048,6144]{1,0:T(8,128)(2,1)}), bf16[256,6144]{1,0:T(8,128)(2,1)}) %reduce-scatter.5.cloned.1.call-update) | async-done | bytes 3145744 | tf_op jit(solution)/shard_map/reduce_scatter | solution.py:986
  889.0 5.0 fusion.20
  (66 shorter events, 30.5 us)
Async XLA Ops:
  7.2 60.4 %all-gather.3.cloned.1.call-start = ((), (), s32[]{:S(2)}) async-start(), calls=%async_computation.2 | async-start | bytes 9437184 | tf_op jit(solution)/shard_map/all_gather | solution.py:982
  9.5 59.2 %copy-start.11 = (f32[128]{0:T(128)S(1)}, f32[128]{0:T(128)}, u32[]{:S(2)}) copy-start(f32[128]{0:T(128)} %constant.26.clone.1) | copy-start | bytes 1540
  9.5 310.9 %all-gather.5.cloned.1.call-start = ((), (), s32[]{:S(2)}) async-start(), calls=%async_computation.3 | async-start | bytes 28311552 | tf_op jit(solution)/shard_map/all_gather | solution.py:982
  67.6 707.2 %reduce-scatter.3.cloned.1.call-start = ((), (), s32[]{:S(2)}) async-start(), calls=%async_computation.4 | async-start | bytes 9437184 | tf_op jit(solution)/shard_map/reduce_scatter | solution.py:986
  69.8 4.8 copy-start.7
  70.0 3.5 copy-start
  74.7 5.8 copy-start.2
  88.7 5.5 copy-start.1
  88.7 5.5 copy-start.8
  106.0 1.1 copy-start.10
  106.3 84.9 %copy-start.3 = (bf16[1024,1024]{1,0:T(8,128)(2,1)}, bf16[1024,1024]{1,0:T(8,128)(2,1)S(1)}, u32[]{:S(2)}) copy-start(bf16[1024,1024]{1,0:T(8,128)(2,1)S(1)} %pad_maximum_fusion.3.k_ref.v_ref.kv_ref) | copy-start | bytes 6291460
  106.3 84.9 %collective-permute-start = (bf16[1024,1024]{1,0:T(8,128)(2,1)S(1)}, bf16[1024,1024]{1,0:T(8,128)(2,1)}, u32[]{:S(2)}, u32[]{:S(2)}) collective-permute-start(bf16[1024,1024]{1,0:T(8,128)(2,1)S(1)} %pad_maximum_fusion.3.k_ref.v_ref.kv_ref), channel_id=1, source_target_pairs={{0,4},{4,0},{1,5},{5,1},{2,6},{6,2},{3,7},{7,3},{8,12},{12,8},{9,1... | collective-permute-start | bytes 6291464 | tf_op jit(solution)/shard_map/ppermute | solution.py:1023
  455.3 24.7 %copy-start.5 = (bf16[2,512,2048]{2,1,0:T(8,128)(2,1)S(1)}, bf16[2,512,2048]{2,1,0:T(8,128)(2,1)}, u32[]{:S(2)}) copy-start(bf16[2,512,2048]{2,1,0:T(8,128)(2,1)} %param.19) | copy-start | bytes 12582916
  493.6 17.7 %copy-start.9 = (bf16[1024,512]{1,0:T(8,128)(2,1)S(1)}, bf16[1024,512]{1,0:T(8,128)(2,1)}, u32[]{:S(2)}) copy-start(bf16[1024,512]{1,0:T(8,128)(2,1)} %get-tuple-element.26.att_ref) | copy-start | bytes 3145732
  657.7 231.3 %reduce-scatter.5.cloned.1.call-start = ((), (), s32[]{:S(2)}) async-start(), calls=%async_computation.5 | async-start | bytes 28311552 | tf_op jit(solution)/shard_map/reduce_scatter | solution.py:986
  889.0 5.0 copy-start.6
  894.0 3.7 copy-start.4
Sparse Core Ops, SparseCore 0:
  10.5 57.0 all-gather.2
  70.0 162.6 all-gather.4
  657.8 70.3 reduce-scatter.2
  732.1 156.8 reduce-scatter.4

commit v2 on v0

--- a/solution.py
+++ b/solution.py
@@ -1,8 +1,12 @@
+import functools
 import math
 
 import jax
 import jax.numpy as jnp
+import numpy as np
 from jax import lax
+from jax.experimental import pallas as pl
+from jax.experimental.pallas import tpu as pltpu
 from jax.sharding import PartitionSpec as P
 
 HD = 128
@@ -62,7 +66,7 @@
     )
 
 
-def body(
+def general_body(
     tokens,
     block_ids,
     query_weight,
@@ -312,6 +316,1217 @@
     )
 
 
+MESH = pl.DeviceIdType.MESH
+ANY = pl.BlockSpec(memory_space=pl.ANY)
+VMEM = pl.BlockSpec(memory_space=pltpu.VMEM)
+BF = jnp.bfloat16
+F32 = jnp.float32
+VMEM_LIMIT = 62 * 1024 * 1024
+CHUNK = 32
+BLOCK_ROWS = 256
+
+
+def params(collective_id=None):
+    if collective_id is None:
+        return pltpu.CompilerParams(vmem_limit_bytes=VMEM_LIMIT)
+    return pltpu.CompilerParams(
+        collective_id=collective_id, has_side_effects=True, vmem_limit_bytes=VMEM_LIMIT
+    )
+
+
+def dot_nt(left, right):
+    return lax.dot_general(left, right, (((1,), (1,)), ((), ())), preferred_element_type=F32)
+
+
+def dot_tn(left, right):
+    return lax.dot_general(left, right, (((0,), (0,)), ((), ())), preferred_element_type=F32)
+
+
+def dot_nn(left, right):
+    return jnp.dot(left, right, preferred_element_type=F32)
+
+
+def rows_of(index, size):
+    return pl.ds(pl.multiple_of(index * size, size), size)
+
+
+def norm_parts(values):
+    centered = values - jnp.mean(values, axis=-1, keepdims=True)
+    inverse = lax.rsqrt(jnp.mean(centered * centered, axis=-1, keepdims=True) + EPSILON)
+    return centered * inverse, inverse
+
+
+class Tree:
+    def __init__(self, chunk, count, acc, from_end, from_mid, out, sems):
+        self.chunk = chunk
+        self.count, self.acc, self.from_end, self.from_mid, self.out = count, acc, from_end, from_mid, out
+        self.slots = acc.shape[0] // chunk
+        self.sent, self.got_end, self.got_mid, self.fin_sent, self.fin_got, self.fin_kept = sems
+        position = lax.axis_index("mp")
+        self.outer = position + 1 - 2 * (position % 2)
+        self.peer = 3 - position
+        self.is_mid = (position + 1) // 2 == 1
+        self.is_end = (position + 1) // 2 != 1
+
+    def barrier(self, beside_seq=False, extra=0):
+        barrier = pltpu.get_barrier_semaphore()
+        pl.semaphore_signal(barrier, inc=1, device_id={"mp": self.outer}, device_id_type=MESH)
+
+        @pl.when(self.is_mid)
+        def _():
+            pl.semaphore_signal(barrier, inc=1, device_id={"mp": self.peer}, device_id_type=MESH)
+
+        position = lax.axis_index("mp")
+        pl.semaphore_wait(barrier, 1 + extra + (position * (3 - position)) // 2)
+
+    def slot(self, j):
+        return rows_of(j % self.slots, self.chunk)
+
+    def part(self, j):
+        return pltpu.make_async_remote_copy(
+            self.acc.at[self.slot(j)], self.from_end.at[self.slot(j)], self.sent.at[j % self.slots], self.got_end.at[j % self.slots],
+            device_id={"mp": self.outer}, device_id_type=MESH,
+        )
+
+    def pair(self, j):
+        return pltpu.make_async_remote_copy(
+            self.acc.at[self.slot(j)], self.from_mid.at[self.slot(j)], self.sent.at[j % self.slots], self.got_mid.at[j % self.slots],
+            device_id={"mp": self.peer}, device_id_type=MESH,
+        )
+
+    def final(self, j):
+        return pltpu.make_async_remote_copy(
+            self.acc.at[self.slot(j)], self.out.at[rows_of(j, self.chunk)], self.fin_sent.at[j % self.slots], self.fin_got.at[j % self.slots],
+            device_id={"mp": self.outer}, device_id_type=MESH,
+        )
+
+    def keep(self, j):
+        return pltpu.make_async_copy(
+            self.acc.at[self.slot(j)], self.out.at[rows_of(j, self.chunk)], self.fin_kept.at[j % self.slots]
+        )
+
+    def send_block(self, block):
+        per_block = BLOCK_ROWS // self.chunk
+
+        @pl.when(self.is_end)
+        def _():
+            for s in range(per_block):
+                self.part(block * per_block + s).start()
+
+    def settle(self, first, amount):
+        @pl.when(self.is_end)
+        def _():
+            def one(s, carry):
+                self.part(first + s).wait_send()
+                self.final(first + s).wait_recv()
+                return carry
+
+            lax.fori_loop(0, amount, one, 0)
+
+        @pl.when(self.is_mid)
+        def _():
+            def one(s, carry):
+                self.final(first + s).wait_send()
+                self.keep(first + s).wait()
+                return carry
+
+            lax.fori_loop(0, amount, one, 0)
+
+    def middle_step(self, i, lag_sum, lag_final, epilogue, first=0, last=None):
+        last = self.count if last is None else last
+        j = i - lag_sum
+
+        @pl.when(self.is_mid & (j >= first) & (j < last))
+        def _():
+            self.part(j).wait_recv()
+            where = self.slot(j)
+            self.acc[where] = (self.acc[where].astype(F32) + self.from_end[where].astype(F32)).astype(BF)
+            self.pair(j).start()
+
+        k = i - lag_final
+
+        @pl.when(self.is_mid & (k >= first) & (k < last))
+        def _():
+            self.pair(k).wait_recv()
+            where = self.slot(k)
+            total = self.acc[where].astype(F32) + self.from_mid[where].astype(F32)
+            result = epilogue(k, total)
+            self.pair(k).wait_send()
+            self.acc[where] = result
+            self.final(k).start()
+            self.keep(k).start()
+
+    def drain(self):
+        self.settle(self.count - self.slots, self.slots)
+
+
+class Feed:
+    def __init__(self, chunk, count, source, slots, sem):
+        self.chunk, self.count, self.source, self.slots, self.sem = chunk, count, source, slots, sem
+
+    def copy(self, j):
+        return pltpu.make_async_copy(
+            self.source.at[rows_of(j, self.chunk)], self.slots.at[j % 2], self.sem.at[j % 2]
+        )
+
+    def begin(self):
+        self.copy(0).start()
+        self.copy(1).start()
+
+    def take(self, j):
+        self.copy(j).wait()
+        return self.slots[j % 2]
+
+    def following(self, j):
+        @pl.when(j + 2 < self.count)
+        def _():
+            self.copy(j + 2).start()
+
+
+class Drop:
+    def __init__(self, chunk, count, target, slots, sem):
+        self.chunk, self.count, self.target, self.slots, self.sem = chunk, count, target, slots, sem
+
+    def copy(self, j):
+        return pltpu.make_async_copy(
+            self.slots.at[j % 2], self.target.at[rows_of(j, self.chunk)], self.sem.at[j % 2]
+        )
+
+    def put(self, j, values):
+        @pl.when(j >= 2)
+        def _():
+            self.copy(j - 2).wait()
+
+        self.slots[j % 2] = values
+        self.copy(j).start()
+
+    def finish(self):
+        self.copy(self.count - 2).wait()
+        self.copy(self.count - 1).wait()
+
+
+def tree_scratch(chunk, held_rows, width):
+    buffers = [pltpu.VMEM((held_rows, width), BF) for _ in range(3)]
+    return buffers + [pltpu.SemaphoreType.DMA((held_rows // chunk,)) for _ in range(6)]
+
+
+class Plane:
+    def __init__(self):
+        dp, self.y = lax.axis_index("dp"), lax.axis_index("seq")
+        self.x, self.core = dp // 2, dp % 2
+        self.sibling = {"dp": self.x * 2 + 1 - self.core}
+        self.x_next = {"dp": (1 - self.x) * 2 + self.core}
+        self.y_next = {"seq": 1 - self.y}
+
+    def greet(self):
+        barrier = pltpu.get_barrier_semaphore()
+        for device in (self.sibling, self.x_next, self.y_next):
+            pl.semaphore_signal(barrier, inc=1, device_id=device, device_id_type=MESH)
+
+    def block_at(self, r, core):
+        over_x, over_y = r // 2, r % 2
+        x = self.x + over_x * (1 - 2 * self.x)
+        y = self.y + over_y * (1 - 2 * self.y)
+        return (x * 2 + core) * 2 + y
+
+
+class Gather:
+    def __init__(self, plane, out, own_rows, width, sent, got):
+        self.plane, self.out, self.own_rows, self.width, self.sent, self.got = plane, out, own_rows, width, sent, got
+
+    def piece(self, m, kind):
+        plane, part = self.plane, self.width // 4
+        r, device, shift, size = (
+            (0, plane.sibling, 0, self.width),
+            (0, plane.x_next, 0, self.width),
+            (0, plane.y_next, 0, self.width),
+            (1, plane.x_next, 0, self.width if self.early(m) else 3 * part),
+            (2, plane.y_next, 3 * part, part),
+            (2, plane.sibling, 0, self.width),
+            (1, plane.sibling, 0, self.width),
+            (3, plane.sibling, 0, self.width),
+        )[kind]
+        at = pl.ds(pl.multiple_of(m * self.width + shift, part), size)
+        window = self.out.at[rows_of(plane.block_at(r, plane.core), BLOCK_ROWS), at]
+        return pltpu.make_async_remote_copy(
+            self.own_rows.at[:, at] if kind < 3 else window, window, self.sent.at[kind, m], self.got.at[kind, m],
+            device_id=device, device_id_type=MESH,
+        )
+
+    def early(self, m):
+        return isinstance(m, int) and m < 4
+
+    def own_x(self, m):
+        self.piece(m, 1).start()
+        self.piece(m, 0).start()
+
+    def own_y(self, m):
+        self.piece(m, 2).start()
+
+    def relay_x(self, m):
+        self.piece(m, 1).wait_recv()
+        if not self.early(m):
+            self.piece(m, 4).start()
+        self.piece(m, 5).start()
+
+    def relay_y(self, m):
+        self.piece(m, 2).wait_recv()
+        self.piece(m, 3).start()
+        self.piece(m, 6).start()
+
+    def corner(self, m):
+        self.piece(m, 3).wait_recv()
+        if not self.early(m):
+            self.piece(m, 4).wait_recv()
+        self.piece(m, 7).start()
+
+    def complete(self, m):
+        for kind in (0, 5, 6, 7):
+            self.piece(m, kind).wait_recv()
+
+    def settle(self, m):
+        for kind in range(8):
+            if kind != 4 or not self.early(m):
+                self.piece(m, kind).wait_send()
+
+
+class Scatter:
+    def __init__(self, plane, count, width, product, out, work, sums, from_x, from_y, buffers):
+        (
+            self.diag_x, self.diag_y, self.staged,
+            self.sib_sent, self.sib_got, self.credit, self.sent, self.got, self.out_sem,
+        ) = buffers
+        self.plane, self.count, self.width, self.product, self.out = plane, count, width, product, out
+        self.work, self.all_sums, self.all_x, self.all_y = work, sums, from_x, from_y
+        self.half = width // 2
+
+    def lanes(self, index, shift=0, size=None):
+        return pl.ds(pl.multiple_of(index * self.width + shift, self.half), self.width if size is None else size)
+
+    def sums(self, k, r, shift=0, size=None):
+        return self.all_sums.at[:, self.lanes((k % 4) * 4 + r, shift, size)]
+
+    def from_x(self, k, shift=0, size=None):
+        return self.all_x.at[(k % 8) // 4, :, self.lanes(k % 4, shift, size)]
+
+    def from_y(self, k, shift=0, size=None):
+        return self.all_y.at[(k % 8) // 4, :, self.lanes(k % 4, shift, size)]
+
+    def to_sibling(self, k):
+        return pltpu.make_async_remote_copy(
+            self.work.at[k % 2], self.work.at[2 + k % 2], self.sib_sent.at[k % 2], self.sib_got.at[k % 2],
+            device_id=self.plane.sibling, device_id_type=MESH,
+        )
+
+    def piece(self, k, kind):
+        half, x_next, y_next = self.half, self.plane.x_next, self.plane.y_next
+        source, target, device = (
+            (self.sums(k, 3, 0, half), self.diag_x.at[k % 8], x_next),
+            (self.sums(k, 3, half, half), self.diag_y.at[k % 8], y_next),
+            (self.sums(k, 2, 0, half), self.from_x(k, 0, half), x_next),
+            (self.sums(k, 1, half, half), self.from_y(k, half, half), y_next),
+            (self.sums(k, 1, 0, half), self.from_y(k, 0, half), y_next),
+            (self.sums(k, 2, half, half), self.from_x(k, half, half), x_next),
+        )[kind]
+        return pltpu.make_async_remote_copy(
+            source, target, self.sent.at[kind, k % 8], self.got.at[kind, k % 8],
+            device_id=device, device_id_type=MESH,
+        )
+
+    def keep(self, k):
+        return pltpu.make_async_copy(self.staged.at[k % 2], self.out.at[:, self.lanes(k)], self.out_sem.at[k % 2])
+
+    def ready(self):
+        for _ in range(2):
+            pl.semaphore_signal(self.credit, inc=1, device_id=self.plane.sibling, device_id_type=MESH)
+
+    def compute(self, k):
+        @pl.when((k >= 2) & (k < self.count))
+        def _():
+            self.to_sibling(k - 2).wait_send()
+
+        @pl.when((k >= 0) & (k < self.count))
+        def _():
+            plane, rows = self.plane, self.staged.shape[1]
+
+            def both(x, core):
+                result = self.product(k, 2 * x + core).astype(BF)
+                over_x = x + plane.x - 2 * x * plane.x
+                return [(2 * over_x + y + plane.y - 2 * y * plane.y, result[y * rows : (y + 1) * rows]) for y in range(2)]
+
+            def theirs(x, carry):
+                for r, values in both(x, 1 - plane.core):
+                    self.work[k % 2, :, self.lanes(r)] = values
+                return carry
+
+            lax.fori_loop(0, 2, theirs, 0)
+            pl.semaphore_wait(self.credit, 1)
+            self.to_sibling(k).start()
+
+            def ours(x, carry):
+                for r, values in both(x, plane.core):
+                    self.sums(k, r)[...] = values
+                return carry
+
+            lax.fori_loop(0, 2, ours, 0)
+
+    def join_cores(self, k):
+        @pl.when((k >= 0) & (k < self.count))
+        def _():
+            self.to_sibling(k).wait_recv()
+
+            def one(r, carry):
+                at = 3 - r
+                self.sums(k, at)[...] = (
+                    self.sums(k, at)[...].astype(F32) + self.work[2 + k % 2, :, self.lanes(at)].astype(F32)
+                ).astype(BF)
+                return carry
+
+            lax.fori_loop(0, 4, one, 0)
+
+            @pl.when(k + 2 < self.count)
+            def _():
+                pl.semaphore_signal(self.credit, inc=1, device_id=self.plane.sibling, device_id_type=MESH)
+
+            for kind in range(4):
+                self.piece(k, kind).start()
+
+    def join_diagonal(self, k):
+        half = self.half
+
+        @pl.when((k >= 0) & (k < self.count))
+        def _():
+            self.piece(k, 0).wait_recv()
+            target = self.sums(k, 1, 0, half)
+            target[...] = (target[...].astype(F32) + self.diag_x[k % 8].astype(F32)).astype(BF)
+            self.piece(k, 4).start()
+            self.piece(k, 1).wait_recv()
+            target = self.sums(k, 2, half, half)
+            target[...] = (target[...].astype(F32) + self.diag_y[k % 8].astype(F32)).astype(BF)
+            self.piece(k, 5).start()
+
+    def finish(self, k):
+        @pl.when((k >= 0) & (k < self.count))
+        def _():
+            for kind in (2, 3, 4, 5):
+                self.piece(k, kind).wait_recv()
+
+            @pl.when(k >= 2)
+            def _():
+                self.keep(k - 2).wait()
+
+            self.staged[k % 2] = (
+                self.sums(k, 0)[...].astype(F32)
+                + self.from_x(k)[...].astype(F32)
+                + self.from_y(k)[...].astype(F32)
+            )
+            self.keep(k).start()
+            for kind in range(6):
+                self.piece(k, kind).wait_send()
+
+    def drain(self):
+        for k in (self.count - 2, self.count - 1):
+            self.keep(k).wait()
+            self.to_sibling(k).wait_send()
+
+
+def scatter_scratch(rows, width):
+    sem = lambda *shape: pltpu.SemaphoreType.DMA(shape)
+    return [
+        pltpu.VMEM((8, rows, width // 2), BF),
+        pltpu.VMEM((8, rows, width // 2), BF),
+        pltpu.VMEM((4, rows, width), F32),
+        sem(2), sem(2), pltpu.SemaphoreType.REGULAR, sem(6, 8), sem(6, 8), sem(2),
+    ]
+
+
+def layer_kernel(
+    chunk, count, groups, heads,
+    tok_ref, q_w, k_w, v_w, o_w, g_w, u_w, d_w, og_ref, ids_ref, cos_ref, sin_ref,
+    full_ref, n1_ref, rows_ref, mid_ref, gm_ref, hid_ref, ggu_ref, part_ref, grads_ref,
+    acc, from_end, from_mid, *rest,
+):
+    sems, rest = rest[:6], rest[6:]
+    (
+        mid_slots, mid_sem, tok_slots, tok_sem, res_slots, res_sem, og_slots, og_sem, gm_sem,
+        wg, wu, wd, load_sem, xs, ogs, in_sem, work, out_sem,
+        n1_sem, w_sem, own, own_sem, q_s, kv_s, kvo_s, att_s, lse_s, kv_sent, kv_got, g_sent, g_got,
+        lhs_sem, rhs_sem, dkv_sent, dkv_got, ready_x, ready_y, rows_s, columns_s, cos_s, sin_s, table_sem,
+    ) = rest[:42]
+    scatter_buffers = rest[42:]
+    hs, gs, us, ps = (work.at[s] for s in range(4))
+    shards = (q_w, k_w, v_w, o_w, g_w, u_w, d_w)
+    wide, hidden = q_w.shape[1], g_w.shape[1]
+    per_sum = count // 4
+    tree = Tree(chunk, count, acc, from_end, from_mid, rows_ref, sems)
+    drop = Drop(chunk, per_sum, mid_ref, mid_slots, mid_sem)
+    tok_feed = Feed(chunk, per_sum, tok_ref, tok_slots, tok_sem)
+    og_feed = Feed(chunk, per_sum, og_ref, og_slots, og_sem)
+    gm_drop = Drop(chunk, per_sum, gm_ref, mid_slots, gm_sem)
+    plane = Plane()
+    gather = Gather(plane, full_ref, own, wide, g_sent, g_got)
+    shard_len = per_sum * chunk // groups
+    per_block = BLOCK_ROWS // chunk
+    blocks = per_sum // per_block
+    group_blocks = blocks // groups
+    pairs = groups * heads
+    tiles = hidden // wide
+    root = 1.0 / math.sqrt(HD)
+    rows = per_sum * chunk
+    own_rows = rows_of(plane.block_at(0, plane.core), BLOCK_ROWS)
+    n1 = wd.at[pl.ds(0, per_sum * chunk)]
+    wbuf = [wu.at[:, pl.ds(hidden - 2 * wide, wide)], wu.at[:, pl.ds(hidden - wide, wide)]]
+
+    def load_tokens(block):
+        return pltpu.make_async_copy(
+            tok_ref.at[rows_of(block, BLOCK_ROWS)], xs.at[block % 2], in_sem.at[0, block % 2]
+        )
+
+    def save_normed(block):
+        where = rows_of(block, BLOCK_ROWS)
+        return pltpu.make_async_copy(n1.at[where], n1_ref.at[where], n1_sem.at[block])
+
+    own_loads, column = [], 0
+    for s, shard in enumerate(shards):
+        size = shard.shape[1]
+        own_loads.append(pltpu.make_async_copy(shard, own.at[:, pl.ds(column, size)], own_sem.at[s]))
+        column += size
+    own_save = pltpu.make_async_copy(own, full_ref.at[own_rows], own_sem.at[len(shards)])
+    feeds = 3 * tiles
+
+    def feed_chunk(n):
+        return 4 + (n % 3) * tiles + n // 3
+
+    def load_weight(m, slot):
+        return pltpu.make_async_copy(full_ref.at[:, pl.ds(m * wide, wide)], wbuf[slot], w_sem.at[slot])
+
+    def load_feed(n, which):
+        m, at = feed_chunk(n), pl.ds(pl.multiple_of((n // 3) * wide, wide), wide)
+        return pltpu.make_async_copy(
+            full_ref.at[:, pl.ds(pl.multiple_of(m * wide, wide), wide)],
+            (wg, wu, wd)[which].at[:, at],
+            load_sem.at[n],
+        )
+
+    def fill(n):
+        gather.complete(feed_chunk(n))
+        for which in range(3):
+            @pl.when(n % 3 == which)
+            def _():
+                load_feed(n, which).start()
+
+    def cross(p, part):
+        at = pl.ds(part * HD, HD)
+        return pltpu.make_async_remote_copy(
+            kv_s.at[p, :, at], kvo_s.at[p, :, at], kv_sent.at[part, p], kv_got.at[part, p],
+            device_id=plane.y_next, device_id_type=MESH,
+        )
+
+    for block in range(2):
+        load_tokens(block).start()
+    for copy in own_loads:
+        copy.start()
+    tables = [
+        pltpu.make_async_copy(source.at[plane.y], target, table_sem.at[s])
+        for s, (source, target) in enumerate(((cos_ref, cos_s), (sin_ref, sin_s)))
+    ]
+    for copy in tables:
+        copy.start()
+    plane.greet()
+    tree.barrier(extra=3)
+    for s in range(4):
+        own_loads[s].wait()
+    gather.own_x(1)
+    gather.own_x(2)
+    for m in (1, 2, 0, 3):
+        gather.own_y(m)
+    for s in range(4, len(shards)):
+        own_loads[s].wait()
+    own_save.start()
+
+    @pl.when(tree.is_mid)
+    def _():
+        tok_feed.begin()
+
+    for group in range(groups):
+        for s, rank in enumerate((plane.y, 1 - plane.y)):
+            ids = ids_ref[group : group + 1, rows_of(rank, shard_len)].astype(F32)
+            columns_s[s, group] = jnp.broadcast_to(ids, (HD, shard_len)).T.astype(BF)
+            if s == 0:
+                rows_s[group] = jnp.broadcast_to(ids, (8, shard_len))
+
+    def allowed(s, group):
+        return columns_s[s, group].astype(F32)[:, :1] <= rows_s[group][:1]
+
+    for block in range(blocks):
+        load_tokens(block).wait()
+        n1[rows_of(block, BLOCK_ROWS)] = norm_parts(xs[block % 2].astype(F32))[0].astype(BF)
+        save_normed(block).start()
+        if block + 2 < blocks:
+            load_tokens(block + 2).start()
+        if block == 1:
+            gather.relay_y(1)
+            gather.relay_x(1)
+    own_save.wait()
+    for copy in tables:
+        copy.wait()
+
+    def turn(values):
+        return values * cos_s[...] + pltpu.roll(values, HD // 2, 1) * sin_s[...]
+
+    def fetch(m, slot):
+        gather.complete(m)
+        load_weight(m, slot).start()
+
+    def project(slot, group, put):
+        lin = dot_nn(n1[rows_of(group, shard_len)], wbuf[slot][...])
+        for head in range(heads):
+            put(group * heads + head, lin[:, head * HD : (head + 1) * HD])
+
+    def put_key(p, values):
+        kv_s[p, :, pl.ds(0, HD)] = turn(values).astype(BF)
+        cross(p, 0).start()
+
+    def put_value(p, values):
+        kv_s[p, :, pl.ds(HD, HD)] = values.astype(BF)
+        cross(p, 1).start()
+
+    def put_query(p, values):
+        q_s[p] = turn(values).astype(BF)
+
+    gather.relay_y(2)
+    gather.relay_x(2)
+    gather.own_x(0)
+    gather.corner(1)
+    gather.relay_y(0)
+    fetch(1, 0)
+    load_weight(1, 0).wait()
+    project(0, 0, put_key)
+    gather.own_x(3)
+    gather.corner(2)
+    gather.relay_y(3)
+    gather.own_x(feed_chunk(0))
+    gather.own_x(feed_chunk(1))
+    fetch(2, 1)
+    load_weight(2, 1).wait()
+    project(1, 0, put_value)
+    for group in range(1, groups):
+        project(0, group, put_key)
+        project(1, group, put_value)
+    gather.own_y(feed_chunk(0))
+    gather.relay_x(0)
+    gather.corner(0)
+    gather.own_x(feed_chunk(2))
+    fetch(0, 0)
+    load_weight(0, 0).wait()
+    for group in range(groups):
+        project(0, group, put_query)
+    gather.relay_x(3)
+    gather.corner(3)
+    gather.own_x(feed_chunk(3))
+    gather.own_y(feed_chunk(1))
+    fetch(3, 1)
+    gather.own_x(feed_chunk(4))
+    gather.own_y(feed_chunk(2))
+    for block in range(blocks):
+        save_normed(block).wait()
+
+    def attend(p):
+        group, head = p // heads, p % heads
+        queries = q_s[p]
+
+        def scores(keys, s):
+            return jnp.where(allowed(s, group), dot_nt(keys, queries) * root, MASKED)
+
+        own_part = scores(kv_s[p, :, pl.ds(0, HD)], 0)
+        cross(p, 0).wait_recv()
+        other = scores(kvo_s[p, :, pl.ds(0, HD)], 1)
+        top = jnp.maximum(jnp.max(own_part, axis=0, keepdims=True), jnp.max(other, axis=0, keepdims=True))
+        own_part, other = jnp.exp(own_part - top), jnp.exp(other - top)
+        total = jnp.sum(own_part, axis=0, keepdims=True) + jnp.sum(other, axis=0, keepdims=True)
+        scale = 1.0 / total
+        mixed = dot_tn(kv_s[p, :, pl.ds(HD, HD)], (own_part * scale).astype(BF))
+        cross(p, 1).wait_recv()
+        mixed = mixed + dot_tn(kvo_s[p, :, pl.ds(HD, HD)], (other * scale).astype(BF))
+        lane = pl.ds(pl.multiple_of(head * HD, HD), HD)
+        att_s[rows_of(group, shard_len), lane] = mixed.T.astype(BF)
+        lse_s[p] = top + jnp.log(total)
+
+    held = tree.slots // per_block
+
+    def project_out(block):
+        acc[rows_of(block % held, BLOCK_ROWS)] = dot_nt(
+            att_s[rows_of(block, BLOCK_ROWS)], wbuf[1][...]
+        ).astype(BF)
+        tree.send_block(block)
+
+    def first_pairs(p, carry):
+        attend(p)
+        return carry
+
+    lax.fori_loop(0, heads, first_pairs, 0)
+    load_weight(3, 1).wait()
+    for block in range(held):
+        project_out(block)
+
+    def first_epilogue(j, total):
+        middle = tok_feed.take(j).astype(F32) + total
+        tok_feed.following(j)
+        drop.put(j, middle)
+        return norm_parts(middle)[0].astype(BF)
+
+    def second_epilogue(j, total):
+        row = j - per_sum
+        residual(j).wait()
+        normed, inverse = norm_parts(res_slots[j % 2])
+        grad_low = og_feed.take(row).astype(F32)
+        spread = total - jnp.mean(total, axis=-1, keepdims=True)
+        grad = grad_low + inverse * (spread - normed * jnp.mean(total * normed, axis=-1, keepdims=True))
+        residual_start(j + 2)
+        og_feed.following(row)
+        gm_drop.put(row, grad)
+        return grad.astype(BF)
+
+    def residual(j):
+        return pltpu.make_async_copy(
+            mid_ref.at[rows_of(j % per_sum, chunk)], res_slots.at[j % 2], res_sem.at[j % 2]
+        )
+
+    def residual_start(j):
+        @pl.when(j < 3 * per_sum)
+        def _():
+            residual(j).start()
+
+        @pl.when((j >= 3 * per_sum) & (j < count))
+        def _():
+            pltpu.make_async_copy(
+                gm_ref.at[rows_of(j % per_sum, chunk)], res_slots.at[j % 2], res_sem.at[j % 2]
+            ).start()
+
+    def third_epilogue(j, total):
+        residual(j).wait()
+        result = (res_slots[j % 2] + total).astype(BF)
+        residual_start(j + 2)
+        return result
+
+    def fourth_epilogue(j, total):
+        row = j - 3 * per_sum
+        normed, inverse = norm_parts(tok_feed.take(row).astype(F32))
+        tok_feed.following(row)
+        spread = total - jnp.mean(total, axis=-1, keepdims=True)
+        grad = inverse * (spread - normed * jnp.mean(total * normed, axis=-1, keepdims=True))
+        residual(j).wait()
+        result = (res_slots[j % 2] + grad).astype(BF)
+        residual_start(j + 2)
+        return result
+
+    def load_block(block):
+        where, slot = rows_of(block, BLOCK_ROWS), block % 2
+        return (
+            pltpu.make_async_copy(rows_ref.at[where], xs.at[slot], in_sem.at[0, slot]),
+            pltpu.make_async_copy(og_ref.at[where], ogs.at[slot], in_sem.at[1, slot]),
+        )
+
+    def store_block(block):
+        where = rows_of(block, BLOCK_ROWS)
+        return (
+            pltpu.make_async_copy(hs, hid_ref.at[where], out_sem.at[0]),
+            pltpu.make_async_copy(gs, ggu_ref.at[where, pl.ds(0, hidden)], out_sem.at[1]),
+            pltpu.make_async_copy(us, ggu_ref.at[where, pl.ds(hidden, hidden)], out_sem.at[2]),
+            pltpu.make_async_copy(ps, part_ref.at[where], out_sem.at[3]),
+        )
+
+    per_feed = hidden // wide
+    starts = (0, 2 * per_feed, 3 * per_feed, 3 * per_feed + 1)
+    lefts = (rows_ref.at[pl.ds(0, rows)], og_ref, rows_ref.at[pl.ds(rows, rows)], n1_ref)
+    dqkv, ga = wd.at[pl.ds(0, rows), pl.ds(0, 3 * wide)], wd.at[pl.ds(0, rows), pl.ds(3 * wide, wide)]
+    rights = (ggu_ref, hid_ref, att_s, dqkv)
+    weights = wu.at[:, pl.ds(0, 3 * wide)]
+
+    def left_copy(p):
+        return pltpu.make_async_copy(lefts[p], wg.at[pl.ds((p % 2) * rows, rows)], lhs_sem.at[p % 2])
+
+    out_weight = pltpu.make_async_copy(
+        full_ref.at[:, pl.ds(3 * wide, wide)], wu.at[:, pl.ds(0, wide)], w_sem.at[0]
+    )
+    head_weights = pltpu.make_async_copy(full_ref.at[:, pl.ds(0, 3 * wide)], weights, w_sem.at[1])
+
+    def phase(k):
+        return sum((k >= start).astype(jnp.int32) for start in starts[1:])
+
+    def right_slot(k):
+        return (rows_of(k % 2, rows), pl.ds(3 * wide, wide))
+
+    def right_copy(k, p):
+        at = pl.ds(pl.multiple_of((k - starts[p]) * wide, wide), wide)
+        return pltpu.make_async_copy(rights[p].at[:, at], wu.at[right_slot(k)], rhs_sem.at[k % 2])
+
+    def right_arrived(k):
+        pltpu.make_async_copy(att_s, wu.at[right_slot(k)], rhs_sem.at[k % 2]).wait()
+
+    def right_start(k):
+        for p in range(4):
+            last = starts[p + 1] if p < 3 else columns
+
+            @pl.when((k >= starts[p]) & (k < last))
+            def _():
+                right_copy(k, p).start()
+
+    def product(k, block_pair):
+        at = rows_of(block_pair, 2 * BLOCK_ROWS)
+        return dot_tn(wg[rows_of(phase(k) % 2, rows), at], wu[right_slot(k)])
+
+    columns = starts[3] + 3
+    scatter = Scatter(plane, columns, wide, product, grads_ref, work, own, xs, ogs, scatter_buffers)
+
+    def load_part(block):
+        return pltpu.make_async_copy(
+            part_ref.at[rows_of(block, BLOCK_ROWS)], acc.at[rows_of(block % held, BLOCK_ROWS)], load_sem.at[0]
+        )
+
+    def far_grads(p, shift):
+        return wd.at[
+            pl.ds(pl.multiple_of(rows + (p // heads) * shard_len, shard_len), shard_len),
+            pl.ds(pl.multiple_of((p % heads) * 2 * HD + shift, 2 * HD), 2 * HD),
+        ]
+
+    def cross_back(p):
+        return pltpu.make_async_remote_copy(
+            far_grads(p, heads * 2 * HD), far_grads(p, 0), dkv_sent.at[p], dkv_got.at[p],
+            device_id=plane.y_next, device_id_type=MESH,
+        )
+
+    def turn_back(values):
+        return values * cos_s[...] - pltpu.roll(values, HD // 2, 1) * sin_s[...]
+
+    def lane(index):
+        return pl.ds(pl.multiple_of(index * HD, HD), HD)
+
+    def group_grads(group):
+        for b in range(group_blocks):
+            at = rows_of(group * group_blocks + b, BLOCK_ROWS)
+            ga[at] = dot_nn(wg[pl.ds(rows + (group * group_blocks + b) * BLOCK_ROWS, BLOCK_ROWS)], wu[:, pl.ds(0, wide)]).astype(BF)
+
+    def pair_back(p):
+        group, head = p // heads, p % heads
+        where = rows_of(group, shard_len)
+        queries, grads = q_s[p], ga[where, lane(head)]
+        weighed = grads.astype(F32) * att_s[where, lane(head)].astype(F32)
+        delta = jnp.sum(weighed.T, axis=0, keepdims=True)
+        turned = jnp.zeros((HD, shard_len), F32)
+        for mine, source in ((False, kvo_s), (True, kv_s)):
+            raw = dot_nt(source[p, :, pl.ds(0, HD)], queries) * root
+            prob = jnp.where(allowed(0 if mine else 1, group), jnp.exp(raw - lse_s[p]), 0.0)
+            gprob = dot_nt(source[p, :, pl.ds(HD, HD)], grads)
+            graw = (prob * (gprob - delta) * root).astype(BF)
+            gkeys = dot_nn(graw, queries).astype(BF)
+            gvalues = dot_nn(prob.astype(BF), grads).astype(BF)
+            if mine:
+                dqkv[where, lane(heads + head)] = gkeys
+                dqkv[where, lane(2 * heads + head)] = gvalues
+            else:
+                target = far_grads(p, heads * 2 * HD)
+                target[:, pl.ds(0, HD)] = gkeys
+                target[:, pl.ds(HD, HD)] = gvalues
+                cross_back(p).start()
+            turned = turned + dot_tn(source[p, :, pl.ds(0, HD)], graw)
+        dqkv[where, lane(head)] = turn_back(turned.T).astype(BF)
+
+    def pair_join(p):
+        group, head = p // heads, p % heads
+        where = rows_of(group, shard_len)
+        cross_back(p).wait_recv()
+        source = far_grads(p, 0)
+        gkeys = dqkv[where, lane(heads + head)].astype(F32) + source[:, pl.ds(0, HD)].astype(F32)
+        gvalues = dqkv[where, lane(2 * heads + head)].astype(F32) + source[:, pl.ds(HD, HD)].astype(F32)
+        dqkv[where, lane(heads + head)] = turn_back(gkeys).astype(BF)
+        dqkv[where, lane(2 * heads + head)] = gvalues.astype(BF)
+        cross_back(p).wait_send()
+
+    def leave(m, carry):
+        gather.settle(m)
+        return carry
+
+    early_sum = scatter_buffers[2]
+    lag = per_block + 1
+    attend_at = lag
+    third_at, fourth_at = attend_at + heads, 2 * per_block + 3
+    feed_at = per_sum
+    turn_at = 2 * per_sum
+
+    def step(i, carry):
+        tree.middle_step(i, 1, 3, first_epilogue, 0, per_sum)
+        tree.middle_step(i, lag, lag + 2, second_epilogue, per_sum, 2 * per_sum)
+        tree.middle_step(i, lag, lag + 2, third_epilogue, 2 * per_sum, 3 * per_sum)
+        tree.middle_step(i, lag, lag + 2, fourth_epilogue, 3 * per_sum, count)
+
+        @pl.when((i >= 7) & (i % 2 == 1))
+        def _():
+            n = (i - 7) // 2
+
+            @pl.when(n + 5 < feeds)
+            def _():
+                gather.own_x(feed_chunk(n + 5))
+
+            @pl.when(n + 3 < feeds)
+            def _():
+                gather.own_y(feed_chunk(n + 3))
+
+            @pl.when(n < feeds)
+            def _():
+                gather.relay_x(feed_chunk(n))
+                gather.relay_y(feed_chunk(n))
+
+            @pl.when((n >= 2) & (n - 2 < feeds))
+            def _():
+                gather.corner(feed_chunk(n - 2))
+
+            @pl.when((n >= 4) & (n - 4 < feeds - 3))
+            def _():
+                fill(n - 4)
+
+        @pl.when((i >= attend_at) & (i < attend_at + heads))
+        def _():
+            attend(heads + i - attend_at)
+
+        @pl.when(i == third_at)
+        def _():
+            tree.settle(0, per_block)
+            project_out(held)
+
+        @pl.when(i == fourth_at)
+        def _():
+            tree.settle(per_block, per_block)
+            project_out(held + 1)
+            for block in range(2):
+                for copy in load_block(block):
+                    copy.start()
+
+        at_feed = i - feed_at
+        block, part = at_feed // per_block, at_feed % per_block
+        slot = block % 2
+        half = per_block // 2
+        running = (at_feed >= 0) & (at_feed < per_sum)
+
+        @pl.when(i == feed_at + half)
+        def _():
+            @pl.when(tree.is_mid)
+            def _():
+                drop.finish()
+                residual_start(per_sum)
+                residual_start(per_sum + 1)
+                og_feed.begin()
+
+        @pl.when(running & (part == 0))
+        def _():
+            for copy in load_block(block):
+                copy.wait()
+
+            @pl.when(block >= 1)
+            def _():
+                for copy in store_block(block - 1):
+                    copy.wait()
+
+        @pl.when(running & (block == 0) & (part < half))
+        def _():
+            @pl.when(part == tiles - 1)
+            def _():
+                for s in range(3):
+                    fill(3 * part + s)
+
+            for s in range(3):
+                load_feed(3 * part + s, s).wait()
+
+        @pl.when(running & (part < half))
+        def _():
+            at = pl.ds(pl.multiple_of(part * wide, wide), wide)
+            gate = dot_nn(xs[slot], wg[:, at])
+            up = dot_nn(xs[slot], wu[:, at])
+            back_value = dot_nn(ogs[slot], wd[:, at])
+            sig = jax.nn.sigmoid(gate)
+            act = gate * sig
+            hs[:, at] = (act * up).astype(BF)
+            gs[:, at] = (back_value * up * sig * (1.0 + gate * (1.0 - sig))).astype(BF)
+            us[:, at] = (back_value * act).astype(BF)
+
+            @pl.when(block == 0)
+            def _():
+                def spread_out(o, carry):
+                    to = rows_of(o, wide)
+                    add = dot_nt(gs[:, at], wg[to, at]) + dot_nt(us[:, at], wu[to, at])
+
+                    @pl.when(part == 0)
+                    def _():
+                        early_sum[o] = add
+
+                    @pl.when(part > 0)
+                    def _():
+                        early_sum[o] = early_sum[o] + add
+
+                    return carry
+
+                lax.fori_loop(0, acc.shape[1] // wide, spread_out, 0)
+
+        @pl.when(running & (part == half - 1))
+        def _():
+            tree.settle((block + held) * per_block, per_block)
+
+            @pl.when(block == 0)
+            def _():
+                for o in range(acc.shape[1] // wide):
+                    acc[pl.ds(0, BLOCK_ROWS), pl.ds(o * wide, wide)] = early_sum[o].astype(BF)
+                tree.send_block(blocks)
+
+        @pl.when(running & (part >= half))
+        def _():
+            at = pl.ds(pl.multiple_of((part - half) * wide, wide), wide)
+
+            @pl.when(block > 0)
+            def _():
+                acc[rows_of(block % held, BLOCK_ROWS), at] = (
+                    dot_nt(gs[...], wg[at, :]) + dot_nt(us[...], wu[at, :])
+                ).astype(BF)
+
+            ps[:, at] = dot_nt(hs[...], wd[at, :]).astype(BF)
+
+        @pl.when(running & (part == per_block - 1))
+        def _():
+            for copy in store_block(block):
+                copy.start()
+
+            @pl.when(block + 2 < blocks)
+            def _():
+                for copy in load_block(block + 2):
+                    copy.start()
+
+            @pl.when(block > 0)
+            def _():
+                tree.send_block(blocks + block)
+
+        late = i - turn_at
+
+        @pl.when(late == 0)
+        def _():
+            for copy in store_block(blocks - 1):
+                copy.wait()
+            lax.fori_loop(4, 4 + feeds, leave, 0)
+            for m in range(4):
+                gather.settle(m)
+            for p in range(pairs):
+                cross(p, 0).wait_send()
+                cross(p, 1).wait_send()
+            scatter.ready()
+            pl.semaphore_signal(ready_x, inc=1, device_id=plane.x_next, device_id_type=MESH)
+            pl.semaphore_signal(ready_y, inc=1, device_id=plane.y_next, device_id_type=MESH)
+            first_rows = pl.ds(0, shard_len)
+            first = pltpu.make_async_copy(
+                lefts[2].at[first_rows], wg.at[pl.ds(rows, shard_len)], lhs_sem.at[1]
+            )
+            first.start()
+            out_weight.start()
+            left_copy(0).start()
+            right_copy(0, 0).start()
+            right_copy(1, 0).start()
+            first.wait()
+            out_weight.wait()
+            group_grads(0)
+            pl.semaphore_wait(ready_x, 1)
+            pl.semaphore_wait(ready_y, 1)
+
+        later = late - 3
+
+        @pl.when((later >= 0) & (later % per_block == 0) & (later < per_sum))
+        def _():
+            block = later // per_block
+            tree.settle((2 * blocks - held + block) * per_block, per_block)
+            load_part(block).start()
+            load_part(block).wait()
+            tree.send_block(2 * blocks + block)
+
+        @pl.when((later >= per_sum) & (later % per_block == 0) & (later < 2 * per_sum))
+        def _():
+            block = later // per_block - blocks
+            tree.settle((3 * blocks - held + block) * per_block, per_block)
+            half = acc.shape[1] // 2
+            for s in range(2):
+                at = pl.ds(s * half, half)
+                acc[rows_of(block % held, BLOCK_ROWS), at] = dot_nt(
+                    dqkv[rows_of(block, BLOCK_ROWS)], wu[at, pl.ds(0, 3 * wide)]
+                ).astype(BF)
+            tree.send_block(3 * blocks + block)
+
+        @pl.when((late >= 1) & (late < 1 + 3 * heads) & ((late - 1) % 3 == 0))
+        def _():
+            pair_back((late - 1) // 3)
+
+        second_at = 3 + per_block + 1
+
+        @pl.when(late == second_at)
+        def _():
+            @pl.when(tree.is_mid)
+            def _():
+                gm_drop.finish()
+                tok_feed.begin()
+
+            second = pltpu.make_async_copy(
+                lefts[2].at[pl.ds(shard_len, rows - shard_len)],
+                wg.at[pl.ds(rows + shard_len, rows - shard_len)],
+                lhs_sem.at[1],
+            )
+            second.start()
+            second.wait()
+            for group in range(1, groups):
+                group_grads(group)
+            left_copy(1).start()
+            head_weights.start()
+
+        more = late - second_at - 1
+
+        @pl.when((more >= 0) & (more < 3 * (pairs - heads)) & (more % 3 == 0))
+        def _():
+            pair_back(heads + more // 3)
+
+        join = late - second_at - 1 - 3 * (pairs - heads) - 1
+
+        @pl.when((join >= 0) & (join < pairs // 2))
+        def _():
+            pair_join(2 * join)
+            pair_join(2 * join + 1)
+
+        @pl.when(join == pairs // 2)
+        def _():
+            head_weights.wait()
+
+        tick = late - 21
+
+        @pl.when((tick >= 0) & (tick % 3 == 0))
+        def _():
+            k = tick // 3
+            scatter.join_cores(k - 1)
+            scatter.join_diagonal(k - 2)
+
+            @pl.when(k < columns)
+            def _():
+                right_arrived(k)
+
+            for p in range(4):
+                @pl.when(k == starts[p])
+                def _():
+                    left_copy(p).wait()
+
+            scatter.compute(k)
+            for p in (2, 3):
+                @pl.when(k == starts[p - 1] - 1)
+                def _():
+                    left_copy(p).start()
+
+            right_start(k + 2)
+            scatter.finish(k - 3)
+
+        return carry
+
+    steps = max(count + lag + 2, turn_at + 21 + 3 * (columns + 2) + 1)
+    lax.fori_loop(0, steps, step, 0)
+    scatter.drain()
+    tree.drain()
+
+
+def layer(tokens, shards, out_grad, block_ids, cosine, sine, groups):
+    rows, model = tokens.shape
+    width, hidden = shards[0].shape[1], shards[-1].shape[1]
+    heads = width // HD
+    pairs = groups * heads
+    shard_len = rows // groups
+    count = 4 * rows // CHUNK
+    total = sum(shard.shape[1] for shard in shards)
+    chunks = total // width
+    sem = lambda *shape: pltpu.SemaphoreType.DMA(shape)
+    shape = jax.ShapeDtypeStruct
+    slots = lambda kind: [pltpu.VMEM((2, CHUNK, model), kind), sem(2)]
+    block = lambda *lead: pltpu.VMEM((*lead, BLOCK_ROWS, model), BF)
+    outs = pl.pallas_call(
+        functools.partial(layer_kernel, CHUNK, count, groups, heads),
+        out_shape=(
+            shape((model, total), BF),
+            shape((rows, model), BF),
+            shape((4 * rows, model), BF),
+            shape((rows, model), F32),
+            shape((rows, model), F32),
+            shape((rows, hidden), BF),
+            shape((rows, 2 * hidden), BF),
+            shape((rows, model), BF),
+            shape((BLOCK_ROWS, total), F32),
+        ),
+        in_specs=[ANY] * 9 + [VMEM] + [ANY] * 2,
+        out_specs=(ANY,) * 9,
+        scratch_shapes=tree_scratch(CHUNK, 2 * BLOCK_ROWS, model)
+        + slots(F32) + slots(BF) + slots(F32) + slots(BF) + [sem(2)]
+        + [pltpu.VMEM((model, hidden), BF) for _ in range(3)]
+        + [sem(3 * hidden // width), block(2), block(2), sem(2, 2), block(4), sem(4)]
+        + [
+            sem(rows // BLOCK_ROWS), sem(2), pltpu.VMEM((BLOCK_ROWS, total), BF), sem(8),
+            pltpu.VMEM((pairs, shard_len, HD), BF),
+            pltpu.VMEM((pairs, shard_len, 2 * HD), BF),
+            pltpu.VMEM((pairs, shard_len, 2 * HD), BF),
+            pltpu.VMEM((rows, width), BF),
+            pltpu.VMEM((pairs, 1, shard_len), F32),
+            sem(2, pairs), sem(2, pairs), sem(8, chunks), sem(8, chunks),
+            sem(2), sem(2), sem(pairs), sem(pairs), pltpu.SemaphoreType.REGULAR, pltpu.SemaphoreType.REGULAR,
+            pltpu.VMEM((groups, 8, shard_len), F32),
+            pltpu.VMEM((2, groups, shard_len, HD), BF),
+            pltpu.VMEM((shard_len, HD), F32),
+            pltpu.VMEM((shard_len, HD), F32),
+            sem(2),
+        ]
+        + scatter_scratch(BLOCK_ROWS, width),
+        compiler_params=params(1),
+    )(tokens, *shards, out_grad, block_ids, cosine, sine)
+    return outs[2], outs[-1]
+
+
+def tree_body(
+    tokens,
+    block_ids,
+    query_weight,
+    key_weight,
+    value_weight,
+    out_weight,
+    gate_weight,
+    up_weight,
+    down_weight,
+    out_grad,
+):
+    groups, shard_len, model = tokens.shape
+    rows = groups * shard_len
+    width, hidden = query_weight.shape[1], gate_weight.shape[1]
+    ranks = lax.axis_size("seq")
+    frequency = np.exp(np.arange(HD // 2) * (-2.0 * math.log(THETA) / HD))
+    angles = np.arange(ranks * shard_len)[:, None] * frequency[None, :]
+    table = lambda *halves: jnp.asarray(
+        np.concatenate(halves, axis=1).reshape(ranks, shard_len, HD).astype(np.float32)
+    )
+    cosine = table(np.cos(angles), np.cos(angles))
+    sine = table(-np.sin(angles), np.sin(angles))
+    flat_tokens = tokens.reshape(rows, model)
+    grad_low = out_grad.reshape(rows, model)
+    shards = (query_weight, key_weight, value_weight, out_weight, gate_weight, up_weight, down_weight)
+    results, grads = layer(
+        flat_tokens, shards, grad_low, block_ids, cosine, sine, groups
+    )
+    at = 3 * hidden + width
+    return (
+        results[2 * rows : 3 * rows].reshape(tokens.shape),
+        results[3 * rows :].reshape(tokens.shape),
+        grads[:, at : at + width],
+        grads[:, at + width : at + 2 * width],
+        grads[:, at + 2 * width :],
+        grads[:, 3 * hidden : at],
+        grads[:, :hidden],
+        grads[:, hidden : 2 * hidden],
+        grads[:, 2 * hidden : 3 * hidden],
+    )
+
+
 def solution(mesh):
     in_specs = (
         P("dp", "seq", None),
@@ -336,4 +1551,6 @@
         P(("dp", "seq"), "mp"),
         P(("dp", "seq"), "mp"),
     )
+    fits = mesh.shape["dp"] == 4 and mesh.shape["seq"] == 2 and mesh.shape["mp"] == 4
+    body = tree_body if fits else general_body
     return jax.shard_map(body, mesh=mesh, in_specs=in_specs, out_specs=out_specs, check_vma=False)

time: 1620 us -> 508 us (0.31)
  waiting for transfers between devices: 1190 us -> 0 us
  Pallas kernels: 0 us -> 492 us
  matrix products: 245 us -> 0 us
  other arithmetic: 91.9 us -> 0 us
  local copies, waits for them, and re-layouts: 65.5 us -> 12.9 us
    psum x3 -> x0, waiting for transfers between devices: 600 us -> none  [the longest x1 292 us: body(): lax.psum(matmul_trans(hidden_low, full_down).astype(jnp.bfloat16), 'mp')]
    pallas_call x0 -> x1, Pallas kernels: none -> 492 us  [layer(): pl.pallas_call(functools.partial(layer_kernel, CHUNK, count, groups, head...]
    reduce_scatter x9 -> x0, waiting for transfers between devices: 346 us -> none  [the longest x1 72.8 us: body(): lax.psum_scatter(grad_terms[4].astype(jnp.bfloat16), ('dp', 'seq'), scatt...]
    dot_general x35 -> x0, matrix products: 245 us -> none  [the longest x7 67.9 us: outer_sum(): lax.dot_general(factor_left, factor_right, (((0,), (0,)), ((), ())), pref...]
    all_gather x9 -> x0, waiting for transfers between devices: 242 us -> none  [the longest x1 44.3 us: body(): lax.all_gather(shards[4], ('dp', 'seq'), axis=0, tiled=True)]
    convert_element_type x15 -> x0, other arithmetic: 41.9 us -> none  [the longest x6 12.8 us: body(): query_grad, key_grad, value_grad, out_weight_grad, gate_grad, up_grad, do...]
    reduce_sum x9 -> x0, other arithmetic: 33.7 us -> none  [the longest x2 15.6 us: norm_back(): middle_term = upstream - jnp.mean(upstream, axis=-1, keepdims=True)]
  transfers between devices with their start and end apart: 21 -> 0, of which waited for: 20 -> 0; matrix products, arithmetic and copies ran while one was open for 15% -> 0% of each run, Pallas kernels for 0% -> 0%
where the time goes in v2:
time: 508 us; the launch traced here: 506 us
  Pallas kernels  492 us (97%)
  local copies, waits for them, and re-layouts  12.9 us (3%)
    pallas_call x1, Pallas kernels, layer(): pl.pallas_call(functools.partial(layer_kernel, CHUNK, count, groups, head...  492 us

profile of v2, /device:TPU:0, one launch (start us, length us, event | category | flops | bytes accessed | tf_op | source)
XLA Modules:
  0.0 505.7 jit_solution(14581073364009223204)
XLA Ops:
  0.6 492.1 %shard_map.187 = (bf16[2048,8192]{1,0:T(8,128)(2,1)}, bf16[1024,2048]{1,0:T(8,128)(2,1)}, bf16[4096,2048]{1,0:T(8,128)(2,1)}, f32[1024,2048]{1,0:T(8,128)}, f32[...) custom-call(bf16[1024,2048]{1,0:T(8,128)(2,1)} %bitcast.4, ...), custom_call_target="tpu_custom_call" | custom-call | tf_op jit(solution)/shard_map/pallas_call | solution.py:1447
  492.8 0.0 copy-start
  492.8 7.1 %fusion = (bf16[1024,2048]{1,0:T(8,128)(2,1)}, bf16[1024,2048]{1,0:T(8,128)(2,1)}) fusion(bf16[4096,2048]{1,0:T(8,128)(2,1)} %get-tuple-element.11), kind=kLoop, calls=%fused_computation | loop fusion | bytes 16777216 | tf_op jit(solution)/shard_map/slice | solution.py:1519
  499.9 1.6 copy-done
  501.5 1.3 fusion.2
  502.9 2.8 fusion.1
Async XLA Ops:
  492.8 8.8 %copy-start = (f32[256,8192]{1,0:T(8,128)S(1)}, f32[256,8192]{1,0:T(8,128)}, u32[]{:S(2)}) copy-start(f32[256,8192]{1,0:T(8,128)} %get-tuple-element.12) | copy-start | bytes 25165828
